TPU v7x, 32 devices: a whole 2x2x4 slice. The times are simulated.
32 devices in a mesh: dp: 4 (over y, x), expert: 8 (over z, core).
Axes of the slice: x: 2, y: 2, z: 4, core: 2. Of those that a mesh axis runs over, the one named last changes fastest.
Arguments:
- tokens: bfloat16 [4096, 768], P(('dp', 'expert')), may hold values from -6 to 6
- expert_ids: int32 [4096, 2], P(('dp', 'expert')), may hold values from 0 to 7, all different within a row; in each aligned block of 128 rows (0 to 127, 128 to 255, ...) at most 64 rows name the same one
- router: bfloat16 [768, 8], replicated, may hold values from -0.4375 to 0.4375
- weight_in: bfloat16 [8, 768, 3072], P('expert'), may hold values from -0.21875 to 0.21875
- weight_out: bfloat16 [8, 3072, 768], P('expert'), may hold values from -0.4375 to 0.4375
- premises: bfloat16 [512, 768], P('dp'), may hold values from -6 to 6
- positive: int32 [64], replicated, may hold values from 0 to 511
- tile_mask: int32 [32, 4], replicated, may hold values 0 or 1
Outputs:
- grad_in: float32 [8, 768, 3072], P('expert', 'dp')
- grad_out: float32 [8, 3072, 768], P('expert', 'dp')
Inputs may be any that keep to these rules, and one draw needn't show every extreme that they name: `expert_ids`: among the 128 tokens of one device no expert is named by more than 64 pairs, and one expert is named by exactly 64; the two experts of a token differ.
All inputs are finite; a program needn't handle non-finite values.
Results may differ from a plain program's by a relative error of at most 0.02.
Values may be sent and summed in bfloat16 or wider, within the bound.
A program may use at most 128 MiB of HBM per device.

v0:
```python
import jax
import jax.numpy as jnp
from jax import lax
from jax.sharding import PartitionSpec as P

LEN = 64


SCORE_SCALE = 20.0
LOSS_SCALE = 64.0
EPSILON = 1e-06


def gelu_parts(pre_act):
    inner_arg = 0.7978845608028654 * (pre_act + 0.044715 * pre_act * pre_act * pre_act)
    tangent = jnp.tanh(inner_arg)
    gelu_val = 0.5 * pre_act * (1.0 + tangent)
    slope_val = 0.5 * (1.0 + tangent) + 0.5 * pre_act * (
        1.0 - tangent * tangent
    ) * 0.7978845608028654 * (1.0 + 0.134145 * pre_act * pre_act)
    return (gelu_val, slope_val)


def route_slots(expert_ids, logits, experts, capacity):
    pick_hot = expert_ids[:, :, None] == jnp.arange(experts, dtype=jnp.int32)[None, None, :]
    picked = jnp.sum(jnp.where(pick_hot, logits[:, None, :], jnp.zeros((), logits.dtype)), axis=2)
    gate_wts = jax.nn.sigmoid(picked - picked[:, ::-1]).astype(jnp.bfloat16)
    flat_ids = expert_ids.reshape(-1)
    flat_hot = (flat_ids[:, None] == jnp.arange(experts, dtype=jnp.int32)[None, :]).astype(
        jnp.int32
    )
    running = jnp.cumsum(flat_hot, axis=0)
    position = jnp.sum(running * flat_hot, axis=1) - 1
    slot_ids = flat_ids * capacity + position
    return (gate_wts, slot_ids.reshape(expert_ids.shape))


def contrast_terms(query_vec, key_rows, key_scale, open_mask, pos_hot):
    include = jnp.logical_or(open_mask, pos_hot)
    scores = (
        SCORE_SCALE
        * lax.dot_general(
            query_vec, key_rows, (((1,), (1,)), ((), ())), preferred_element_type=jnp.float32
        )
        * key_scale[None, :]
    )
    exp_scores = jnp.where(include, jnp.exp(scores), jnp.zeros((), scores.dtype))
    partition = jnp.sum(exp_scores, axis=1)
    soft_weight = (exp_scores * key_scale[None, :]).astype(jnp.bfloat16)
    weighted_sum = jnp.dot(soft_weight, key_rows, preferred_element_type=jnp.float32)
    pos_scale = jnp.sum(
        jnp.where(pos_hot, key_scale[None, :], jnp.zeros((), key_scale.dtype)), axis=1
    )
    pos_vec = (
        jnp.dot(pos_hot.astype(jnp.bfloat16), key_rows, preferred_element_type=jnp.float32)
        * pos_scale[:, None]
    )
    return (weighted_sum, partition, pos_vec)


def on_device(tokens, expert_ids, router, weight_in, weight_out, premises, positive, tile_mask):
    token_count, model_width = tokens.shape
    ffn_width = weight_in.shape[2]
    experts = router.shape[1]
    expert_size = lax.axis_size("expert")
    capacity = 4 * token_count // expert_size
    slot_total = experts * capacity
    dp_index = lax.axis_index("dp")
    col_index = lax.axis_index("expert")
    device = dp_index * expert_size + col_index
    logits = jnp.dot(tokens, router, preferred_element_type=jnp.float32)
    gate_wts, slot_ids = route_slots(expert_ids, logits, experts, capacity)
    slot_hot = slot_ids[:, :, None] == jnp.arange(slot_total, dtype=jnp.int32)[None, None, :]
    placing = jnp.sum(slot_hot.astype(jnp.bfloat16), axis=1)
    combine = jnp.sum(
        jnp.where(slot_hot, gate_wts[:, :, None], jnp.zeros((), jnp.bfloat16)), axis=1
    )
    outgoing = lax.dot_general(
        placing, tokens, (((0,), (0,)), ((), ())), preferred_element_type=jnp.float32
    ).astype(jnp.bfloat16)
    outgoing = outgoing.reshape(experts, capacity, model_width)
    arrived = lax.all_to_all(outgoing, "expert", split_axis=0, concat_axis=0, tiled=True)
    sources = arrived.shape[0]
    slot_count = arrived.shape[1]
    flat_in = arrived.reshape(sources * slot_count, model_width)
    pre_act = jnp.dot(flat_in, weight_in[0], preferred_element_type=jnp.float32)
    gelu_val, slope_val = gelu_parts(pre_act)
    hidden = gelu_val.astype(jnp.bfloat16)
    result = jnp.dot(hidden, weight_out[0], preferred_element_type=jnp.float32).astype(jnp.bfloat16)
    returned = lax.all_to_all(
        result.reshape(sources, slot_count, model_width),
        "expert",
        split_axis=0,
        concat_axis=0,
        tiled=True,
    )
    received, hidden, slope_val, returned = (
        arrived,
        hidden.reshape(sources, slot_count, ffn_width),
        slope_val.reshape(sources, slot_count, ffn_width),
        returned,
    )
    mixed_out = tokens.astype(jnp.float32) + jnp.dot(
        combine, returned.reshape(slot_total, model_width), preferred_element_type=jnp.float32
    )
    seq_count = token_count // LEN
    pooled = jnp.sum(mixed_out.reshape(seq_count, LEN, model_width), axis=1) / LEN
    row_scale = lax.rsqrt(jnp.sum(pooled * pooled, axis=1) + EPSILON)
    unit_vec = pooled * row_scale[:, None]
    query_vec = unit_vec.astype(jnp.bfloat16)
    prem_count = premises.shape[0]
    key_rows = lax.all_gather(premises, "dp", axis=0, tiled=True)
    key_scale = lax.rsqrt(jnp.sum(jnp.square(key_rows.astype(jnp.float32)), axis=1) + EPSILON)
    key_index = jnp.arange(key_rows.shape[0], dtype=jnp.int32)
    own_positive = lax.dynamic_slice_in_dim(positive, device * seq_count, seq_count)
    mask_row = lax.dynamic_index_in_dim(tile_mask, device, 0, keepdims=False)
    key_open = jnp.repeat(mask_row, prem_count) == 1
    weighted_sum, partition, pos_vec = contrast_terms(
        query_vec,
        key_rows,
        key_scale,
        key_open[None, :],
        key_index[None, :] == own_positive[:, None],
    )
    delta_unit = LOSS_SCALE * SCORE_SCALE * (weighted_sum / partition[:, None] - pos_vec)
    delta_pooled = row_scale[:, None] * (
        delta_unit - unit_vec * jnp.sum(unit_vec * delta_unit, axis=1, keepdims=True)
    )
    delta_mixed = jnp.broadcast_to(
        delta_pooled[:, None, :] / LEN, (seq_count, LEN, model_width)
    ).reshape(token_count, model_width)
    grad_send = lax.dot_general(
        combine.astype(jnp.float32),
        delta_mixed,
        (((0,), (0,)), ((), ())),
        precision=lax.Precision.HIGHEST,
        preferred_element_type=jnp.float32,
    ).astype(jnp.bfloat16)
    grad_recv = lax.all_to_all(
        grad_send.reshape(experts, capacity, model_width),
        "expert",
        split_axis=0,
        concat_axis=0,
        tiled=True,
    )
    grad_flat = grad_recv.reshape(-1, model_width)
    row_total = grad_flat.shape[0]
    hidden_flat = hidden.reshape(row_total, ffn_width)
    slope_flat = slope_val.reshape(row_total, ffn_width)
    input_flat = received.reshape(row_total, model_width)
    grad_out_term = lax.dot_general(
        hidden_flat, grad_flat, (((0,), (0,)), ((), ())), preferred_element_type=jnp.float32
    )
    dhidden = lax.dot_general(
        grad_flat, weight_out[0], (((1,), (1,)), ((), ())), preferred_element_type=jnp.float32
    )
    delta_pre = (dhidden * slope_flat).astype(jnp.bfloat16)
    grad_in_term = lax.dot_general(
        input_flat, delta_pre, (((0,), (0,)), ((), ())), preferred_element_type=jnp.float32
    )
    grad_in, grad_out = (
        lax.psum_scatter(
            grad_in_term[None].astype(jnp.bfloat16), "dp", scatter_dimension=1, tiled=True
        ).astype(jnp.float32),
        lax.psum_scatter(
            grad_out_term[None].astype(jnp.bfloat16), "dp", scatter_dimension=1, tiled=True
        ).astype(jnp.float32),
    )
    return (grad_in, grad_out)


def solution(mesh):
    in_specs = (
        P(("dp", "expert"), None),
        P(("dp", "expert"), None),
        P(),
        P("expert", None, None),
        P("expert", None, None),
        P("dp", None),
        P(),
        P(),
    )
    out_specs = (P("expert", "dp", None), P("expert", "dp", None))
    return jax.shard_map(
        on_device, mesh=mesh, in_specs=in_specs, out_specs=out_specs, check_vma=False
    )
```

profile of v0, /device:TPU:0, one launch (start us, length us, event | category | flops | bytes accessed | tf_op | source)
XLA Modules:
  0.0 237.5 jit_solution(7114610421702368181)
XLA Ops:
  7.2 0.0 copy-start
  7.2 0.8 copy.24
  8.0 0.1 eq.85
  8.1 0.1 eq.81
  8.3 0.6 reduce-window.6
  8.9 0.2 slice_reduce_fusion
  9.1 0.1 fusion.27
  9.2 0.1 sub.19
  9.4 0.1 copy.26
  9.4 0.7 multiply_add_fusion.1
  10.1 0.0 copy-done
  10.1 1.0 fusion.39
  11.2 0.8 select_reduce_fusion
  12.0 0.2 fusion.26
  12.2 1.3 convolution_convert_fusion.3
  13.5 27.1 %all_to_all.15 = bf16[8,64,768]{2,1,0:T(8,128)(2,1)S(1)} all-to-all(bf16[8,64,768]{2,1,0:T(8,128)(2,1)S(1)} %bitcast.52), channel_id=1, replica_groups=mesh['dp'=4,'expert'=8] {'expert'}, dimensions={0} | all-to-all | bytes 1572864 | tf_op jit(solution)/shard_map/all_to_all | solution.py:82
  40.6 0.0 slice-start
  40.6 0.0 slice-start.1
  40.6 4.6 %fusion.10 = f32[512,3072]{1,0:T(8,128)S(1)} fusion(bf16[512,768]{1,0:T(8,128)(2,1)S(1)} %bitcast.48, bf16[1,768,3072]{2,1,0:T(8,128)(2,1)} %param.11), kind=kOutput, calls=%fused_computation.15 | convolution fusion | flops 2415919104 | bytes 11796480 | tf_op jit(solution)/shard_map/dot_general | solution.py:86
  45.2 0.0 slice-done
  45.2 0.0 slice-done.1
  45.2 0.0 copy-start.1
  45.2 0.0 copy-start.5
  45.2 0.0 copy-start.4
  45.3 0.0 copy-start.3
  45.3 0.0 copy-start.2
  45.3 4.7 %fusion.16 = bf16[512,768]{1,0:T(8,128)(2,1)} fusion(bf16[1,3072,768]{2,1,0:T(8,128)(2,1)S(1)} %bitcast.57, f32[512,3072]{1,0:T(8,128)S(1)} %fusion.10), kind=kOutput, calls=%fused_computation.20 | convolution fusion | flops 2430468096 | bytes 11796480 | tf_op jit(solution)/shard_map/dot_general | solution.py:89
  50.0 0.0 copy-done.1
  50.0 3.5 %all-to-all-start.1 = ((bf16[8,64,768]{2,1,0:T(8,128)(2,1)}), bf16[8,64,768]{2,1,0:T(8,128)(2,1)S(1)}, u32[]{:S(2)}, u32[]{:S(2)}) async-start(bf16[8,64,768]{2,1,0:T(8,128)(2,1)} %bitcast.6), calls=%async_computation.1 | async-start | bytes 1572864 | tf_op jit(solution)/shard_map/all_to_all | solution.py:90
  53.5 0.0 reduce-scatter.3.cloned.1.call-start
  53.6 0.0 copy-done.5
  53.6 0.1 dynamic_slice.8
  53.7 0.0 copy-done.4
  53.7 0.2 fusion.31
  53.9 0.0 copy-done.3
  53.9 12.5 %all_gather.3 = bf16[512,768]{1,0:T(8,128)(2,1)S(1)} all-gather(bf16[128,768]{1,0:T(8,128)(2,1)S(1)} %copy-done.3), channel_id=1, replica_groups=mesh['dp'=4,'expert'=8] {'dp'}, dimensions={0}, use_global_device_ids=true | all-gather | bytes 983040 | tf_op jit(solution)/shard_map/all_gather | solution.py:112
  66.4 0.2 multiply_reduce_fusion
  66.6 0.2 select_reduce_fusion.1
  66.8 0.1 broadcast_bitcast_fusion
  66.9 7.6 %all-to-all-done.1 = bf16[8,64,768]{2,1,0:T(8,128)(2,1)S(1)} async-done(((bf16[8,64,768]{2,1,0:T(8,128)(2,1)}), bf16[8,64,768]{2,1,0:T(8,128)(2,1)S(1)}, u32[]{:S(2)}, u32[]{:S(2)}) %all-to-all-start.1) | async-done | bytes 786464 | tf_op jit(solution)/shard_map/all_to_all | solution.py:90
  74.4 0.0 copy-done.2
  74.4 0.3 bitcast_reduce_fusion
  74.7 0.1 multiply_reduce_fusion.2
  74.8 0.4 fusion.38
  75.3 0.2 convolution_divide_fusion
  75.5 0.4 multiply_reduce_fusion.1
  75.9 0.1 multiply_multiply_fusion.1
  76.0 0.8 convolution_convert_fusion.2
  76.9 23.4 %all_to_all.16 = bf16[8,64,768]{2,1,0:T(8,128)(2,1)S(1)} all-to-all(bf16[8,64,768]{2,1,0:T(8,128)(2,1)S(1)} %bitcast.51), channel_id=1, replica_groups=mesh['dp'=4,'expert'=8] {'expert'}, dimensions={0} | all-to-all | bytes 1572864 | tf_op jit(solution)/shard_map/all_to_all | solution.py:139
  100.2 11.3 %fusion.12 = bf16[1,768,3072]{2,1,0:T(8,128)(2,1)} fusion(bf16[512,768]{1,0:T(8,128)(2,1)S(1)} %bitcast.49, f32[512,3072]{1,0:T(8,128)} %copy-done.1, bf16[512,768]{1,0:T(8,128)(2,1)S(1)} %bitcast.54, bf16[1,3072,768]{2,1,0:T(8,128)(2,1)} %param.12), kind=kOutput, calls=%fused_computation.17 | convolution fusion | flops 4864081920 | bytes 17301504 | tf_op jit(solution)/shard_map/dot_general | solution.py:158
  111.6 0.0 reduce-scatter.3.cloned.1.call-update
  111.6 0.2 reduce-scatter.5.cloned.1.call-start
  111.8 8.3 %fusion.13 = bf16[1,3072,768]{2,1,0:T(8,128)(2,1)} fusion(bf16[512,768]{1,0:T(8,128)(2,1)S(1)} %bitcast.55, f32[512,3072]{1,0:T(8,128)} %copy-done.1), kind=kOutput, calls=%fused_computation.18 | convolution fusion | flops 2432434176 | bytes 11796480 | tf_op jit(solution)/shard_map/dot_general | solution.py:151
  120.2 0.0 reduce-scatter.5.cloned.1.call-update
  120.2 47.6 %reduce-scatter.3.cloned.1.call-done = bf16[1,192,3072]{2,1,0:T(8,128)(2,1)} async-done(((bf16[1,768,3072]{2,1,0:T(8,128)(2,1)}), bf16[1,192,3072]{2,1,0:T(8,128)(2,1)}) %reduce-scatter.3.cloned.1.call-update) | async-done | bytes 1179664 | tf_op jit(solution)/shard_map/reduce_scatter | solution.py:162
  167.7 2.9 %convert_element_type.76 = f32[1,192,3072]{2,1,0:T(8,128)} convert(bf16[1,192,3072]{2,1,0:T(8,128)(2,1)} %reduce-scatter.3.cloned.1.call-done) | non-fusion elementwise | flops 589824 | bytes 3538944 | tf_op jit(solution)/shard_map/convert_element_type | solution.py:164
  170.7 57.2 %reduce-scatter.5.cloned.1.call-done = bf16[1,768,768]{2,1,0:T(8,128)(2,1)} async-done(((bf16[1,3072,768]{2,1,0:T(8,128)(2,1)}), bf16[1,768,768]{2,1,0:T(8,128)(2,1)}) %reduce-scatter.5.cloned.1.call-update) | async-done | bytes 1179664 | tf_op jit(solution)/shard_map/reduce_scatter | solution.py:165
  227.9 2.8 %convert_element_type.79 = f32[1,768,768]{2,1,0:T(8,128)} convert(bf16[1,768,768]{2,1,0:T(8,128)(2,1)} %reduce-scatter.5.cloned.1.call-done) | non-fusion elementwise | flops 589824 | bytes 3538944 | tf_op jit(solution)/shard_map/convert_element_type | solution.py:167
  (10 shorter events, 0.1 us)
Async XLA Ops:
  7.2 3.0 %copy-start = (bf16[768,8]{0,1:T(8,128)(2,1)S(1)}, bf16[768,8]{0,1:T(8,128)(2,1)}, u32[]{:S(2)}) copy-start(bf16[768,8]{0,1:T(8,128)(2,1)} %param.10) | copy-start | bytes 36868
  40.6 4.6 %slice-start = ((s8[4718592]{0:T(1024)(128)(4,1)}), s8[4194304]{0:T(1024)(128)(4,1)S(1)}, s32[]{:S(2)}) async-start(s8[4718592]{0:T(1024)(128)(4,1)} %bitcast.56), calls=%async_computation.7 | async-start | bytes 8388608
  40.6 4.6 %slice-start.1 = ((s8[4718592]{0:T(1024)(128)(4,1)}), s8[524288]{0:T(1024)(128)(4,1)S(1)}, s32[]{:S(2)}) async-start(s8[4718592]{0:T(1024)(128)(4,1)} %bitcast.56), calls=%async_computation.8 | async-start | bytes 1048576
  45.2 4.7 %copy-start.1 = (f32[512,3072]{1,0:T(8,128)}, f32[512,3072]{1,0:T(8,128)S(1)}, u32[]{:S(2)}) copy-start(f32[512,3072]{1,0:T(8,128)S(1)} %fusion.10) | copy-start | bytes 18874372
  45.2 8.3 %copy-start.5 = (s32[64]{0:T(128)S(1)}, s32[64]{0:T(128)}, u32[]{:S(2)}) copy-start(s32[64]{0:T(128)} %param.14) | copy-start | bytes 772
  45.2 8.4 %copy-start.4 = (s32[32,4]{0,1:T(4,128)S(1)}, s32[32,4]{0,1:T(4,128)}, u32[]{:S(2)}) copy-start(s32[32,4]{0,1:T(4,128)} %param.15) | copy-start | bytes 1540
  45.3 8.6 %copy-start.3 = (bf16[128,768]{1,0:T(8,128)(2,1)S(1)}, bf16[128,768]{1,0:T(8,128)(2,1)}, u32[]{:S(2)}) copy-start(bf16[128,768]{1,0:T(8,128)(2,1)} %param.13) | copy-start | bytes 589828
  45.3 29.2 %copy-start.2 = (bf16[128,768]{1,0:T(8,128)(2,1)S(1)}, bf16[128,768]{1,0:T(8,128)(2,1)}, u32[]{:S(2)}) copy-start(bf16[128,768]{1,0:T(8,128)(2,1)} %param.8) | copy-start | bytes 589828
  50.0 24.5 %all-to-all-start.1 = ((bf16[8,64,768]{2,1,0:T(8,128)(2,1)}), bf16[8,64,768]{2,1,0:T(8,128)(2,1)S(1)}, u32[]{:S(2)}, u32[]{:S(2)}) async-start(bf16[8,64,768]{2,1,0:T(8,128)(2,1)} %bitcast.6), calls=%async_computation.1 | async-start | bytes 1572864 | tf_op jit(solution)/shard_map/all_to_all | solution.py:90
  53.5 114.2 %reduce-scatter.3.cloned.1.call-start = ((), (), s32[]{:S(2)}) async-start(), calls=%async_computation.5 | async-start | bytes 5898240 | tf_op jit(solution)/shard_map/reduce_scatter | solution.py:162
  111.6 116.3 %reduce-scatter.5.cloned.1.call-start = ((), (), s32[]{:S(2)}) async-start(), calls=%async_computation.6 | async-start | bytes 5898240 | tf_op jit(solution)/shard_map/reduce_scatter | solution.py:165
Sparse Core Ops, SparseCore 0:
  111.7 55.9 reduce-scatter.2
  170.7 57.0 reduce-scatter.4
where the time goes:
time: 238 us
  waiting for transfers between devices  112 us (47%)
  blocking collectives  63 us (26%)
  matrix products  33.5 us (14%)
  between operations  14.2 us (6%)
  other arithmetic  8.97 us (4%)
  starting transfers between devices  3.81 us (2%)
    reduce_scatter x1, waiting for transfers between devices, on_device(): lax.psum_scatter(grad_out_term[None].astype(jnp.bfloat16), 'dp', scatter_...  57.2 us
    reduce_scatter x1, waiting for transfers between devices, on_device(): lax.psum_scatter(grad_in_term[None].astype(jnp.bfloat16), 'dp', scatter_d...  47.6 us
    all_to_all x1, blocking collectives, on_device(): lax.all_to_all(outgoing, 'expert', split_axis=0, concat_axis=0, tiled=True)  27.1 us
    all_to_all x1, blocking collectives, on_device(): lax.all_to_all(grad_send.reshape(experts, capacity, model_width), 'expert...  23.4 us
    all_gather x1, blocking collectives, on_device(): key_rows = lax.all_gather(premises, 'dp', axis=0, tiled=True)  12.5 us
    dot_general x1, matrix products, on_device(): lax.dot_general(input_flat, delta_pre, (((0,), (0,)), ((), ())), preferre...  11.3 us
    dot_general x1, matrix products, on_device(): lax.dot_general(hidden_flat, grad_flat, (((0,), (0,)), ((), ())), preferr...  8.35 us
    all_to_all x1, waiting for transfers between devices, on_device(): lax.all_to_all(result.reshape(sources, slot_count, model_width), 'expert'...  7.55 us
  transfers between devices with their start and end apart: 3, of which 3 were waited for; matrix products, arithmetic and copies ran while one was open for 5% of the time, Pallas kernels for 0%

commit v1 on v0

v1 whole, which is shorter than its diff:
```python
import jax
import jax.numpy as jnp
from jax import lax
from jax.sharding import PartitionSpec as P

LEN = 64
SCORE_SCALE = 20.0
LOSS_SCALE = 64.0
EPSILON = 1e-06
AXES = ("dp", "expert")


def gelu_parts(pre_act):
    inner_arg = 0.7978845608028654 * (pre_act + 0.044715 * pre_act * pre_act * pre_act)
    tangent = jnp.tanh(inner_arg)
    gelu_val = 0.5 * pre_act * (1.0 + tangent)
    slope_val = 0.5 * (1.0 + tangent) + 0.5 * pre_act * (
        1.0 - tangent * tangent
    ) * 0.7978845608028654 * (1.0 + 0.134145 * pre_act * pre_act)
    return (gelu_val, slope_val)


def gate_map(tokens, expert_ids, router):
    logits = jnp.dot(tokens, router, preferred_element_type=jnp.float32)
    experts = router.shape[1]
    hot = expert_ids[:, :, None] == jnp.arange(experts, dtype=jnp.int32)[None, None, :]
    picked = jnp.sum(jnp.where(hot, logits[:, None, :], 0.0), axis=2)
    gate = jax.nn.sigmoid(picked - picked[:, ::-1])
    return jnp.sum(jnp.where(hot, gate[:, :, None], 0.0), axis=1).T.astype(jnp.bfloat16)


def on_device(tokens, expert_ids, router, weight_in, weight_out, premises, positive, tile_mask):
    bf16, f32 = jnp.bfloat16, jnp.float32
    token_count, width = tokens.shape
    experts = router.shape[1]
    n_dp, n_ex = lax.axis_size("dp"), lax.axis_size("expert")
    blocks = n_dp * n_ex
    capacity = 4 * token_count // n_ex
    ff = weight_in.shape[2] // n_dp
    dp, ex = lax.axis_index("dp"), lax.axis_index("expert")
    device = dp * n_ex + ex
    per_dev = token_count // LEN
    seqs = blocks * per_dev

    gates = lax.all_gather(gate_map(tokens, expert_ids, router), AXES, axis=0)
    all_tokens = lax.all_gather(tokens, AXES, axis=0)
    keys = lax.all_gather(premises, "dp", axis=0, tiled=True)

    gate = lax.dynamic_index_in_dim(gates, ex, 1, keepdims=False)
    named = gate != 0
    upper = (jnp.arange(token_count)[:, None] <= jnp.arange(token_count)[None, :]).astype(bf16)
    place_at = jnp.dot(named.astype(bf16), upper, preferred_element_type=f32).astype(jnp.int32) - 1
    place = jnp.logical_and(
        place_at[:, None, :] == jnp.arange(capacity, dtype=jnp.int32)[None, :, None], named[:, None, :]
    )
    rows = lax.dot_general(
        place.astype(bf16), all_tokens, (((2,), (1,)), ((0,), (0,))), preferred_element_type=f32
    ).astype(bf16).reshape(blocks * capacity, width)
    own_seq = (jnp.arange(token_count) // LEN)[:, None] == jnp.arange(per_dev)[None, :]
    slot_gate = jnp.sum(
        jnp.where(
            jnp.logical_and(place[:, :, :, None], own_seq[None, None]),
            gate.astype(f32)[:, None, :, None],
            0.0,
        ),
        axis=2,
    )
    eye = jnp.eye(blocks, dtype=f32)
    spread = (slot_gate[:, :, None, :] * eye[:, None, :, None]).astype(bf16).reshape(
        blocks * capacity, seqs
    )

    w_in = lax.dynamic_slice_in_dim(weight_in[0], dp * ff, ff, 1)
    w_out = lax.dynamic_slice_in_dim(weight_out[0], dp * ff, ff, 0)
    pre_act = jnp.dot(rows, w_in, preferred_element_type=f32)
    gelu_val, slope_val = gelu_parts(pre_act)
    hidden = gelu_val.astype(bf16)
    seq_hidden = lax.dot_general(
        spread, hidden, (((0,), (0,)), ((), ())), preferred_element_type=f32
    ).astype(bf16)
    partial = jnp.dot(seq_hidden, w_out, preferred_element_type=f32)
    own_sum = jnp.sum(tokens.astype(f32).reshape(per_dev, LEN, width), axis=1)
    mine = (jnp.arange(seqs) // per_dev == device)[:, None]
    partial = partial + jnp.where(mine, jnp.tile(own_sum, (blocks, 1)), 0.0)
    pooled = lax.psum(partial, AXES) / LEN

    row_scale = lax.rsqrt(jnp.sum(pooled * pooled, axis=1) + EPSILON)
    unit = pooled * row_scale[:, None]
    key_scale = lax.rsqrt(jnp.sum(jnp.square(keys.astype(f32)), axis=1) + EPSILON)
    pos_hot = jnp.arange(keys.shape[0], dtype=jnp.int32)[None, :] == positive[:, None]
    key_open = jnp.repeat(jnp.repeat(tile_mask, premises.shape[0], axis=1), per_dev, axis=0) == 1
    include = jnp.logical_or(key_open, pos_hot)
    scores = SCORE_SCALE * lax.dot_general(
        unit.astype(bf16), keys, (((1,), (1,)), ((), ())), preferred_element_type=f32
    ) * key_scale[None, :]
    exp_scores = jnp.where(include, jnp.exp(scores), 0.0)
    partition = jnp.sum(exp_scores, axis=1)
    soft = (exp_scores * key_scale[None, :]).astype(bf16)
    both = jnp.dot(
        jnp.concatenate([soft, pos_hot.astype(bf16)], axis=0), keys, preferred_element_type=f32
    )
    pos_scale = jnp.sum(jnp.where(pos_hot, key_scale[None, :], 0.0), axis=1)
    delta_unit = LOSS_SCALE * SCORE_SCALE * (
        both[:seqs] / partition[:, None] - both[seqs:] * pos_scale[:, None]
    )
    delta = row_scale[:, None] * (
        delta_unit - unit * jnp.sum(unit * delta_unit, axis=1, keepdims=True)
    )
    delta = (delta / LEN).astype(bf16)

    grad_out = lax.dot_general(
        seq_hidden, delta, (((0,), (0,)), ((), ())), preferred_element_type=f32
    )
    seq_dh = lax.dot_general(
        delta, w_out, (((1,), (1,)), ((), ())), preferred_element_type=f32
    ).astype(bf16)
    delta_pre = (jnp.dot(spread, seq_dh, preferred_element_type=f32) * slope_val).astype(bf16)
    grad_in = lax.dot_general(
        rows, delta_pre, (((0,), (0,)), ((), ())), preferred_element_type=f32
    ).astype(bf16)
    grad_in = lax.all_to_all(grad_in, "dp", split_axis=0, concat_axis=1, tiled=True)
    return (grad_in.astype(f32)[None], grad_out[None])


def solution(mesh):
    in_specs = (
        P(AXES, None),
        P(AXES, None),
        P(),
        P("expert", None, None),
        P("expert", None, None),
        P("dp", None),
        P(),
        P(),
    )
    out_specs = (P("expert", "dp", None), P("expert", "dp", None))
    return jax.shard_map(
        on_device, mesh=mesh, in_specs=in_specs, out_specs=out_specs, check_vma=False
    )
```

time: 238 us -> 272 us (1.14)
  waiting for transfers between devices: 112 us -> 145 us
  local copies, waits for them, and re-layouts: 1.75 us -> 4.94 us
    psum x0 -> x1, waiting for transfers between devices: none -> 122 us  [on_device(): pooled = lax.psum(partial, AXES) / LEN]
    reduce_scatter x2 -> x0, waiting for transfers between devices: 105 us -> none  [the longest x1 57.2 us: on_device(): lax.psum_scatter(grad_out_term[None].astype(jnp.bfloat16), 'dp', scatter_...]
    all_gather x1 -> x2, blocking collectives: 12.5 us -> 63.3 us  [the longest x1 43.8 us: on_device(): gates = lax.all_gather(gate_map(tokens, expert_ids, router), AXES, axis=0)]
    all_to_all x2 -> x0, blocking collectives: 50.5 us -> none  [the longest x1 27.1 us: on_device(): lax.all_to_all(outgoing, 'expert', split_axis=0, concat_axis=0, tiled=True)]
    all_gather x0 -> x1, waiting for transfers between devices: none -> 10.1 us  [on_device(): all_tokens = lax.all_gather(tokens, AXES, axis=0)]
    all_to_all x1, waiting for transfers between devices: 7.55 us -> 12.8 us  [on_device(): lax.all_to_all(grad_in, 'dp', split_axis=0, concat_axis=1, tiled=True)]
    convert_element_type x0 -> x3, local copies, waits for them, and re-layouts: none -> 4.23 us  [the longest x2 3.78 us: on_device(): return (grad_in.astype(f32)[None], grad_out[None])]
    convert_element_type x4 -> x6, other arithmetic: 5.8 us -> 2.23 us  [the longest x1 1.07 us: on_device(): delta = (delta / LEN).astype(bf16)]
  transfers between devices with their start and end apart: 3 -> 3, of which waited for: 3 -> 3; matrix products, arithmetic and copies ran while one was open for 5% -> 3% of each run, Pallas kernels for 0% -> 0%
where the time goes in v1:
time: 272 us; the launch traced here: 271 us
  waiting for transfers between devices  145 us (53%)
  blocking collectives  63.3 us (23%)
  matrix products  31.5 us (12%)
  between operations  14.3 us (5%)
  other arithmetic  8.07 us (3%)
  local copies, waits for them, and re-layouts  4.94 us (2%)
  starting transfers between devices  3.6 us (1%)
    psum x1, waiting for transfers between devices, on_device(): pooled = lax.psum(partial, AXES) / LEN  122 us
    all_gather x1, blocking collectives, on_device(): gates = lax.all_gather(gate_map(tokens, expert_ids, router), AXES, axis=0)  43.8 us
    all_gather x1, blocking collectives, on_device(): keys = lax.all_gather(premises, 'dp', axis=0, tiled=True)  19.5 us
    all_to_all x1, waiting for transfers between devices, on_device(): lax.all_to_all(grad_in, 'dp', split_axis=0, concat_axis=1, tiled=True)  12.8 us
    dot_general x1, matrix products, on_device(): lax.dot_general(rows, delta_pre, (((0,), (0,)), ((), ())), preferred_elem...  11.4 us
    all_gather x1, waiting for transfers between devices, on_device(): all_tokens = lax.all_gather(tokens, AXES, axis=0)  10.1 us
  transfers between devices with their start and end apart: 3, of which 3 were waited for; matrix products, arithmetic and copies ran while one was open for 3% of the time, Pallas kernels for 0%

profile of v1, /device:TPU:0, one launch (start us, length us, event | category | flops | bytes accessed | tf_op | source)
XLA Modules:
  0.0 271.0 jit_solution(6355669295784010667)
XLA Ops:
  7.2 0.0 copy-start
  7.2 0.0 all-gather.4.cloned.1.call-start
  7.2 0.7 all-gather.4.cloned.1.call-update
  7.9 0.0 all-reduce.2.cloned.1.call-start
  8.0 0.0 copy-done
  8.0 1.0 fusion.56
  9.0 0.8 select_reduce_fusion.3
  9.8 0.7 select_reduce_fusion.2
  10.5 43.8 %all-gather = bf16[256,128]{1,0:T(8,128)(2,1)S(1)} all-gather(bf16[8,128]{1,0:T(8,128)(2,1)S(1)} %bitcast.66), channel_id=2, replica_groups=mesh['dp'=4,'expert'=8] {'dp','expert'}, dimensions={0}, use_global_device_ids=true | all-gather | bytes 67584 | tf_op jit(solution)/shard_map/all_gather | solution.py:45
  54.4 1.0 convert_reduce_fusion
  55.4 0.1 tile.4
  55.4 0.1 tile.10
  55.6 0.1 fusion.26
  55.7 0.2 fusion.27
  56.0 0.7 select_reduce_fusion
  56.7 0.2 multiply_convert_fusion.4
  56.9 0.5 convert_element_type.94
  57.4 19.5 %all_gather.19 = bf16[512,768]{1,0:T(8,128)(2,1)S(1)} all-gather(bf16[128,768]{1,0:T(8,128)(2,1)} %param.13), channel_id=1, replica_groups=mesh['dp'=4,'expert'=8] {'dp'}, dimensions={0}, use_global_device_ids=true | all-gather | bytes 983040 | tf_op jit(solution)/shard_map/all_gather | solution.py:47
  76.8 0.2 multiply_reduce_fusion
  77.1 0.7 fusion.36
  77.8 10.1 %all-gather.4.cloned.1.call-done = bf16[4096,768]{1,0:T(8,128)(2,1)} async-done(((bf16[128,768]{1,0:T(8,128)(2,1)}), bf16[4096,768]{1,0:T(8,128)(2,1)}) %all-gather.4.cloned.1.call-update) | async-done | bytes 6291472 | tf_op jit(solution)/shard_map/all_gather | solution.py:46
  87.9 3.8 %convolution_convert_fusion = bf16[32,64,768]{2,1,0:T(8,128)(2,1)S(1)} fusion(bf16[32,128,768]{2,1,0:T(8,128)(2,1)} %bitcast.55, s32[32,128]{1,0:T(8,128)S(1)} %fusion.26, pred[32,128]{1,0:T(8,128)(4,1)S(1)} %bitcast.62), kind=kOutput, calls=%fused_computation.13 | convolution fusion | flops 404750336 | bytes 9457664 | tf_op jit(solution)/shard_map/dot_general | solution.py:56
  91.7 0.0 copy-start.1
  91.7 4.9 %fusion.14 = f32[2048,768]{1,0:T(8,128)S(1)} fusion(bf16[2048,768]{1,0:T(8,128)(2,1)S(1)} %bitcast.56, bf16[1,768,3072]{2,1,0:T(8,128)(2,1)} %param.11, s32[]{:T(128)S(6)} %select_n.55), kind=kOutput, calls=%fused_computation.22 | convolution fusion | flops 2415919104 | bytes 10616836 | tf_op jit(solution)/shard_map/dot_general | solution.py:75
  96.6 0.0 copy-done.1
  96.7 0.0 copy-start.4
  96.7 0.0 copy-start.3
  96.7 0.0 copy-start.2
  96.7 2.5 fusion.23
  99.2 0.1 copy-done.4
  99.3 2.3 fusion.17
  101.6 0.0 all-reduce.2.cloned.1.call-update
  101.6 0.0 copy-done.3
  101.7 0.1 copy.23
  101.8 0.1 broadcast_in_dim.71
  101.9 0.1 broadcast_in_dim.72
  102.0 0.1 eq.106
  102.0 121.7 %all-reduce.2.cloned.1.call-done = f32[64,768]{1,0:T(8,128)} async-done(((f32[64,768]{1,0:T(8,128)}), f32[64,768]{1,0:T(8,128)}) %all-reduce.2.cloned.1.call-update) | async-done | bytes 196624 | tf_op jit(solution)/shard_map/psum | solution.py:85
  223.7 1.0 multiply_reduce_fusion.2
  224.8 0.0 copy-done.2
  224.8 1.4 fusion.55
  226.2 0.3 fusion.32
  226.5 1.2 multiply_reduce_fusion.1
  227.7 1.1 multiply_convert_fusion.5
  228.7 1.8 fusion.20
  230.5 11.4 %fusion.9 = bf16[768,768]{1,0:T(8,128)(2,1)} fusion(bf16[2048,768]{1,0:T(8,128)(2,1)} %bitcast.57, f32[2048,768]{1,0:T(8,128)} %copy-done.4, bf16[2048,64]{0,1:T(8,128)(2,1)S(1)} %convert_element_type.94, bf16[64,768]{1,0:T(8,128)(2,1)S(1)} %fusion.20), kind=kOutput, calls=%fused_computation.17 | convolution fusion | flops 2647719936 | bytes 10977280 | tf_op jit(solution)/shard_map/dot_general | solution.py:118
  242.0 3.5 %all-to-all-start = ((bf16[4,192,768]{2,1,0:T(8,128)(2,1)}), bf16[4,192,768]{2,1,0:T(8,128)(2,1)S(1)}, u32[]{:S(2)}, u32[]{:S(2)}) async-start(bf16[4,192,768]{2,1,0:T(8,128)(2,1)} %bitcast.8), calls=%async_computation | async-start | bytes 2359296 | tf_op jit(solution)/shard_map/all_to_all | solution.py:121
  245.5 1.9 convolution_bitcast_fusion
  247.4 12.8 %all-to-all-done = bf16[4,192,768]{2,1,0:T(8,128)(2,1)S(1)} async-done(((bf16[4,192,768]{2,1,0:T(8,128)(2,1)}), bf16[4,192,768]{2,1,0:T(8,128)(2,1)S(1)}, u32[]{:S(2)}, u32[]{:S(2)}) %all-to-all-start) | async-done | bytes 1179680 | tf_op jit(solution)/shard_map/all_to_all | solution.py:121
  260.2 0.2 convert_bitcast_fusion
  260.4 1.5 copy.24
  261.9 2.3 reshape.135
  (14 shorter events, 0.2 us)
Async XLA Ops:
  7.2 0.8 copy-start
  7.2 80.8 %all-gather.4.cloned.1.call-start = ((), (), s32[]{:S(2)}) async-start(), calls=%async_computation.2 | async-start | bytes 6488064 | tf_op jit(solution)/shard_map/all_gather | solution.py:46
  7.9 215.8 %all-reduce.2.cloned.1.call-start = ((), (), s32[]{:S(2)}) async-start(), calls=%async_computation.1 | async-start | bytes 393216 | tf_op jit(solution)/shard_map/psum | solution.py:85
  91.7 5.0 %copy-start.1 = (bf16[32,64,768]{2,1,0:T(8,128)(2,1)}, bf16[32,64,768]{2,1,0:T(8,128)(2,1)S(1)}, u32[]{:S(2)}) copy-start(bf16[32,64,768]{2,1,0:T(8,128)(2,1)S(1)} %convolution_convert_fusion) | copy-start | bytes 9437188
  96.7 2.7 copy-start.4
  96.7 5.0 %copy-start.3 = (s32[32,4]{0,1:T(4,128)S(1)}, s32[32,4]{0,1:T(4,128)}, u32[]{:S(2)}) copy-start(s32[32,4]{0,1:T(4,128)} %param.15) | copy-start | bytes 1540
  96.7 128.1 %copy-start.2 = (s32[64]{0:T(128)S(1)}, s32[64]{0:T(128)}, u32[]{:S(2)}) copy-start(s32[64]{0:T(128)} %param.14) | copy-start | bytes 772
  242.0 18.2 %all-to-all-start = ((bf16[4,192,768]{2,1,0:T(8,128)(2,1)}), bf16[4,192,768]{2,1,0:T(8,128)(2,1)S(1)}, u32[]{:S(2)}, u32[]{:S(2)}) async-start(bf16[4,192,768]{2,1,0:T(8,128)(2,1)} %bitcast.8), calls=%async_computation | async-start | bytes 2359296 | tf_op jit(solution)/shard_map/all_to_all | solution.py:121
Sparse Core Ops, SparseCore 0:
  11.0 76.8 all-gather.3
  101.8 121.9 all-reduce.1

commit v2 on v1

v2 whole, which is shorter than its diff:
```python
import functools

import jax
import jax.numpy as jnp
from jax import lax
from jax.experimental import pallas as pl
from jax.experimental.pallas import tpu as pltpu
from jax.sharding import PartitionSpec as P

LEN = 64
SCORE_SCALE = 20.0
LOSS_SCALE = 64.0
EPSILON = 1e-06
AXES = ("dp", "expert")


def gelu_parts(pre_act):
    inner_arg = 0.7978845608028654 * (pre_act + 0.044715 * pre_act * pre_act * pre_act)
    tangent = jnp.tanh(inner_arg)
    gelu_val = 0.5 * pre_act * (1.0 + tangent)
    slope_val = 0.5 * (1.0 + tangent) + 0.5 * pre_act * (
        1.0 - tangent * tangent
    ) * 0.7978845608028654 * (1.0 + 0.134145 * pre_act * pre_act)
    return (gelu_val, slope_val)


MESH = pl.DeviceIdType.MESH


def greet_all(n_ex, blocks, me):
    barrier = pltpu.get_barrier_semaphore()

    def hello(d, _):
        t = lax.rem(me + d, blocks)
        pl.semaphore_signal(barrier, inc=1, device_id=(t // n_ex, lax.rem(t, n_ex)), device_id_type=MESH)
        return 0

    lax.fori_loop(1, blocks, hello, 0)
    pl.semaphore_wait(barrier, blocks - 1)


def gather_kernel(n_dp, n_ex, tok, tok_v, ids, router, prem, all_tok, gates, keys,
                  gmap, local_sem, send_sem, core_sem, recv_sem, gsend_sem, grecv_sem, psend_sem, precv_sem):
    blocks, nz = n_dp * n_ex, n_ex // 2
    i, e = lax.axis_index("dp"), lax.axis_index("expert")
    z, c = e // 2, lax.rem(e, 2)
    me, other = i * n_ex + e, z * 2 + (1 - c)

    def at_block(ii, zz, cc):
        return ii * n_ex + zz * 2 + cc

    def move(src, block, sem, device):
        return pltpu.make_async_remote_copy(
            src_ref=src, dst_ref=all_tok.at[block], send_sem=sem, recv_sem=recv_sem.at[block],
            device_id=device, device_id_type=MESH)

    greet_all(n_ex, blocks, me)

    own = pltpu.make_async_copy(tok, all_tok.at[me], local_sem.at[0])
    own.start()
    own_keys = pltpu.make_async_copy(prem, keys.at[i], local_sem.at[1])
    own_keys.start()

    def own_dp(d, _):
        move(tok, me, send_sem.at[0, d], (lax.rem(i + d, n_dp), e)).start()
        return 0

    def own_z(k, _):
        move(tok, me, send_sem.at[k, 0], (i, lax.rem(z + k, nz) * 2 + c)).start()
        return 0

    lax.fori_loop(1, n_dp, own_dp, 0)
    lax.fori_loop(1, nz, own_z, 0)
    move(tok, me, core_sem.at[me], (i, other)).start()

    experts = router.shape[0]
    logits = lax.dot_general(
        router[...], tok_v[...], (((1,), (1,)), ((), ())), preferred_element_type=jnp.float32)
    lane = lax.broadcasted_iota(jnp.int32, logits.shape, 0)
    hot0, hot1 = lane == ids[0:1, :], lane == ids[1:2, :]
    picked0 = jnp.sum(jnp.where(hot0, logits, 0.0), axis=0, keepdims=True)
    picked1 = jnp.sum(jnp.where(hot1, logits, 0.0), axis=0, keepdims=True)
    gate0, gate1 = jax.nn.sigmoid(picked0 - picked1), jax.nn.sigmoid(picked1 - picked0)
    table = jnp.where(hot0, gate0, jnp.where(hot1, gate1, 0.0)).astype(jnp.bfloat16).astype(jnp.float32)
    for k in range(experts):
        gmap[k] = jnp.broadcast_to(table[k:k + 1, :], gmap.shape[1:])

    def gate_copy(d):
        t = lax.rem(me + d, blocks)
        return pltpu.make_async_remote_copy(
            src_ref=gmap.at[lax.rem(t, n_ex)], dst_ref=gates.at[me], send_sem=gsend_sem.at[d],
            recv_sem=grecv_sem.at[me], device_id=(t // n_ex, lax.rem(t, n_ex)), device_id_type=MESH)

    def gate_start(d, _):
        gate_copy(d).start()
        return 0

    lax.fori_loop(1, blocks, gate_start, 0)
    own_gate = pltpu.make_async_copy(gmap.at[e], gates.at[me], local_sem.at[2])
    own_gate.start()

    def from_z(k, _):
        block = at_block(i, lax.rem(z + k, nz), c)
        move(tok, block, send_sem.at[0, 0], (i, e)).wait_recv()

        def on(d, _):
            move(all_tok.at[block], block, send_sem.at[k, d], (lax.rem(i + d, n_dp), e)).start()
            return 0

        lax.fori_loop(1, n_dp, on, 0)
        move(all_tok.at[block], block, core_sem.at[block], (i, other)).start()
        return 0

    lax.fori_loop(1, nz, from_z, 0)

    def half(src, row, part, sem, device):
        return pltpu.make_async_remote_copy(
            src_ref=src, dst_ref=keys.at[row, part], send_sem=psend_sem.at[sem],
            recv_sem=precv_sem.at[row, part], device_id=device, device_id_type=MESH)

    def own_half(d, _):
        half(prem.at[c], i, c, d, (lax.rem(i + d, n_dp), e)).start()
        return 0

    lax.fori_loop(1, n_dp, own_half, 0)

    def from_dp(n, _):
        k, d = n // (n_dp - 1), 1 + lax.rem(n, n_dp - 1)
        block = at_block(lax.rem(i + d, n_dp), lax.rem(z + k, nz), c)
        move(tok, block, send_sem.at[0, 0], (i, e)).wait_recv()
        move(all_tok.at[block], block, core_sem.at[block], (i, other)).start()
        return 0

    lax.fori_loop(0, nz * (n_dp - 1), from_dp, 0)

    def hand_half(d, _):
        row = lax.rem(i + d, n_dp)
        half(prem.at[c], row, c, d, (i, e)).wait_recv()
        half(keys.at[row, c], row, c, n_dp + d, (i, other)).start()
        return 0

    lax.fori_loop(1, n_dp, hand_half, 0)

    own.wait()
    own_keys.wait()
    own_gate.wait()

    def end_core(n, _):
        ii, zz = n // nz, lax.rem(n, nz)
        move(tok, at_block(ii, zz, 1 - c), send_sem.at[0, 0], (i, e)).wait_recv()
        move(tok, me, core_sem.at[at_block(ii, zz, c)], (i, e)).wait_send()
        return 0

    lax.fori_loop(0, n_dp * nz, end_core, 0)

    def end_send(n, _):
        move(tok, me, send_sem.at[n // n_dp, lax.rem(n, n_dp)], (i, e)).wait_send()
        return 0

    lax.fori_loop(1, nz * n_dp, end_send, 0)

    def end_half(d, _):
        half(prem.at[c], lax.rem(i + d, n_dp), 1 - c, d, (i, e)).wait_recv()
        half(prem.at[c], i, c, d, (i, e)).wait_send()
        half(prem.at[c], i, c, n_dp + d, (i, e)).wait_send()
        return 0

    lax.fori_loop(1, n_dp, end_half, 0)

    def end_gate(d, _):
        s = lax.rem(me + d, blocks)
        gate_copy(d).wait_send()
        pltpu.make_async_remote_copy(
            src_ref=gmap.at[0], dst_ref=gates.at[s], send_sem=gsend_sem.at[d],
            recv_sem=grecv_sem.at[s], device_id=(i, e), device_id_type=MESH).wait_recv()
        return 0

    lax.fori_loop(1, blocks, end_gate, 0)


def gather(n_dp, n_ex, tokens, ids, router, premises):
    blocks = n_dp * n_ex
    tok, width = tokens.shape
    prem = premises.reshape(2, premises.shape[0] // 2, width)
    any_spec, vmem = pl.BlockSpec(memory_space=pl.ANY), pl.BlockSpec(memory_space=pltpu.VMEM)
    dma = pltpu.SemaphoreType.DMA
    return pl.pallas_call(
        functools.partial(gather_kernel, n_dp, n_ex),
        out_shape=(
            jax.ShapeDtypeStruct((blocks, tok, width), tokens.dtype),
            jax.ShapeDtypeStruct((blocks, 8, tok), jnp.float32),
            jax.ShapeDtypeStruct((n_dp,) + prem.shape, premises.dtype),
        ),
        in_specs=[any_spec, vmem, vmem, vmem, any_spec],
        out_specs=(any_spec, any_spec, any_spec),
        scratch_shapes=[
            pltpu.VMEM((router.shape[1], 8, tok), jnp.float32),
            dma((3,)), dma((n_ex // 2, n_dp)), dma((blocks,)), dma((blocks,)),
            dma((blocks,)), dma((blocks,)), dma((2 * n_dp,)), dma((n_dp, 2)),
        ],
        compiler_params=pltpu.CompilerParams(collective_id=0, has_side_effects=True),
    )(tokens, tokens, ids.T, router.T, prem)


def loss_kernel(n_dp, n_ex, partial, own_sum, keys, key_scale, include, pos_hot, out,
                inbox, ssend, srecv, gsend, grecv):
    blocks = n_dp * n_ex
    i, e = lax.axis_index("dp"), lax.axis_index("expert")
    me = i * n_ex + e
    per_dev, width = own_sum.shape

    def copy(src, dst, slot, send, recv, t, s):
        return pltpu.make_async_remote_copy(
            src_ref=src, dst_ref=dst.at[slot], send_sem=send.at[s], recv_sem=recv.at[slot],
            device_id=(t // n_ex, lax.rem(t, n_ex)), device_id_type=MESH)

    greet_all(n_ex, blocks, me)

    def scatter(d, _):
        t = lax.rem(me + d, blocks)
        copy(partial.at[t], inbox, me, ssend, srecv, t, d).start()
        return 0

    lax.fori_loop(1, blocks, scatter, 0)

    def collect(d, total):
        s = lax.rem(me + d, blocks)
        copy(partial.at[me], inbox, s, ssend, srecv, me, d).wait_recv()
        return total + inbox[s]

    total = lax.fori_loop(1, blocks, collect, partial[me] + own_sum[...])
    pad = include.shape[0]
    pooled = jnp.concatenate([total, jnp.zeros((pad - per_dev, width), jnp.float32)], axis=0) / LEN
    row_scale = lax.rsqrt(jnp.sum(pooled * pooled, axis=1, keepdims=True) + EPSILON)
    unit = pooled * row_scale
    rows = keys[...]
    scores = SCORE_SCALE * lax.dot_general(
        unit.astype(jnp.bfloat16), rows, (((1,), (1,)), ((), ())), preferred_element_type=jnp.float32
    ) * key_scale[...]
    exp_scores = jnp.where(include[...] > 0, jnp.exp(scores), 0.0)
    partition = jnp.sum(exp_scores, axis=1, keepdims=True)
    soft = (exp_scores * key_scale[...]).astype(jnp.bfloat16)
    weighted = jnp.dot(soft, rows, preferred_element_type=jnp.float32)
    hot = pos_hot[...]
    pos_vec = jnp.dot(hot.astype(jnp.bfloat16), rows, preferred_element_type=jnp.float32)
    pos_scale = jnp.sum(hot * key_scale[...], axis=1, keepdims=True)
    delta_unit = LOSS_SCALE * SCORE_SCALE * (weighted / partition - pos_vec * pos_scale)
    delta = row_scale * (delta_unit - unit * jnp.sum(unit * delta_unit, axis=1, keepdims=True))
    out[me] = delta[:per_dev] / LEN

    def spread(d, _):
        t = lax.rem(me + d, blocks)
        copy(out.at[me], out, me, gsend, grecv, t, d).start()
        return 0

    lax.fori_loop(1, blocks, spread, 0)

    def end(d, _):
        s = lax.rem(me + d, blocks)
        copy(out.at[me], out, s, gsend, grecv, me, d).wait_recv()
        copy(out.at[me], out, me, gsend, grecv, s, d).wait_send()
        copy(partial.at[s], inbox, me, ssend, srecv, s, d).wait_send()
        return 0

    lax.fori_loop(1, blocks, end, 0)


def loss_grads(n_dp, n_ex, partial, own_sum, keys, key_scale, include, pos_hot):
    blocks = n_dp * n_ex
    vmem = pl.BlockSpec(memory_space=pltpu.VMEM)
    dma = pltpu.SemaphoreType.DMA
    return pl.pallas_call(
        functools.partial(loss_kernel, n_dp, n_ex),
        out_shape=jax.ShapeDtypeStruct(partial.shape, jnp.float32),
        in_specs=[vmem] * 6,
        out_specs=vmem,
        scratch_shapes=[
            pltpu.VMEM(partial.shape, jnp.float32),
            dma((blocks,)), dma((blocks,)), dma((blocks,)), dma((blocks,)),
        ],
        compiler_params=pltpu.CompilerParams(
            collective_id=1, has_side_effects=True, vmem_limit_bytes=48 * 1024 * 1024),
    )(partial, own_sum, keys, key_scale, include, pos_hot)


def on_device(tokens, expert_ids, router, weight_in, weight_out, premises, positive, tile_mask):
    bf16, f32 = jnp.bfloat16, jnp.float32
    token_count, width = tokens.shape
    n_dp, n_ex = lax.axis_size("dp"), lax.axis_size("expert")
    blocks = n_dp * n_ex
    capacity = 4 * token_count // n_ex
    ff = weight_in.shape[2] // n_dp
    dp, ex = lax.axis_index("dp"), lax.axis_index("expert")
    device = dp * n_ex + ex
    per_dev = token_count // LEN
    seqs = blocks * per_dev

    all_tokens, gates, keys = gather(n_dp, n_ex, tokens, expert_ids, router, premises)
    keys = keys.reshape(n_dp * premises.shape[0], width)

    gate = gates[:, 0, :]
    named = gate != 0
    upper = (jnp.arange(token_count)[:, None] <= jnp.arange(token_count)[None, :]).astype(bf16)
    place_at = jnp.dot(named.astype(bf16), upper, preferred_element_type=f32).astype(jnp.int32) - 1
    place = jnp.logical_and(
        place_at[:, None, :] == jnp.arange(capacity, dtype=jnp.int32)[None, :, None], named[:, None, :]
    )
    rows = lax.dot_general(
        place.astype(bf16), all_tokens, (((2,), (1,)), ((0,), (0,))), preferred_element_type=f32
    ).astype(bf16).reshape(blocks * capacity, width)
    own_seq = (jnp.arange(token_count) // LEN)[:, None] == jnp.arange(per_dev)[None, :]
    slot_gate = jnp.sum(
        jnp.where(
            jnp.logical_and(place[:, :, :, None], own_seq[None, None]),
            gate[:, None, :, None],
            0.0,
        ),
        axis=2,
    )
    eye = jnp.eye(blocks, dtype=f32)
    spread = (slot_gate[:, :, None, :] * eye[:, None, :, None]).astype(bf16).reshape(
        blocks * capacity, seqs
    )

    w_in = lax.dynamic_slice_in_dim(weight_in[0], dp * ff, ff, 1)
    w_out = lax.dynamic_slice_in_dim(weight_out[0], dp * ff, ff, 0)
    pre_act = jnp.dot(rows, w_in, preferred_element_type=f32)
    gelu_val, slope_val = gelu_parts(pre_act)
    hidden = gelu_val.astype(bf16)
    seq_hidden = lax.dot_general(
        spread, hidden, (((0,), (0,)), ((), ())), preferred_element_type=f32
    ).astype(bf16)
    partial = jnp.dot(seq_hidden, w_out, preferred_element_type=f32)
    own_sum = jnp.sum(tokens.astype(f32).reshape(per_dev, LEN, width), axis=1)
    key_scale = lax.rsqrt(jnp.sum(jnp.square(keys.astype(f32)), axis=1) + EPSILON)
    own_positive = lax.dynamic_slice_in_dim(positive, device * per_dev, per_dev)
    mask_row = lax.dynamic_index_in_dim(tile_mask, device, 0, keepdims=False)
    pos_hot = jnp.arange(keys.shape[0], dtype=jnp.int32)[None, :] == own_positive[:, None]
    include = jnp.logical_or(jnp.repeat(mask_row, premises.shape[0])[None, :] == 1, pos_hot)
    fill = ((0, 16 - per_dev), (0, 0))
    delta = loss_grads(
        n_dp, n_ex, partial.reshape(blocks, per_dev, width), own_sum, keys, key_scale[None, :],
        jnp.pad(include.astype(f32), fill), jnp.pad(pos_hot.astype(f32), fill),
    ).reshape(seqs, width).astype(bf16)

    grad_out = lax.dot_general(
        seq_hidden, delta, (((0,), (0,)), ((), ())), preferred_element_type=f32
    )
    seq_dh = lax.dot_general(
        delta, w_out, (((1,), (1,)), ((), ())), preferred_element_type=f32
    ).astype(bf16)
    delta_pre = (jnp.dot(spread, seq_dh, preferred_element_type=f32) * slope_val).astype(bf16)
    grad_in = lax.dot_general(
        rows, delta_pre, (((0,), (0,)), ((), ())), preferred_element_type=f32
    ).astype(bf16)
    grad_in = lax.all_to_all(grad_in, "dp", split_axis=0, concat_axis=1, tiled=True)
    return (grad_in.astype(f32)[None], grad_out[None])


def solution(mesh):
    in_specs = (
        P(AXES, None),
        P(AXES, None),
        P(),
        P("expert", None, None),
        P("expert", None, None),
        P("dp", None),
        P(),
        P(),
    )
    out_specs = (P("expert", "dp", None), P("expert", "dp", None))
    return jax.shard_map(
        on_device, mesh=mesh, in_specs=in_specs, out_specs=out_specs, check_vma=False
    )
```

time: 272 us -> 142 us (0.52)
  waiting for transfers between devices: 145 us -> 13.7 us
  Pallas kernels: 0 us -> 80.6 us
  blocking collectives: 63.3 us -> 0 us
  between operations: 14.3 us -> 0.83 us
  matrix products: 31.5 us -> 26.9 us
  local copies, waits for them, and re-layouts: 4.94 us -> 9.34 us
    psum x1 -> x0, waiting for transfers between devices: 122 us -> none  [on_device(): pooled = lax.psum(partial, AXES) / LEN]
    pallas_call x0 -> x2, Pallas kernels: none -> 80.6 us  [the longest x1 54.4 us: gather(): pl.pallas_call(functools.partial(gather_kernel, n_dp, n_ex), out_shape=(j...]
    all_gather x2 -> x0, blocking collectives: 63.3 us -> none  [the longest x1 43.8 us: on_device(): gates = lax.all_gather(gate_map(tokens, expert_ids, router), AXES, axis=0)]
    all_gather x1 -> x0, waiting for transfers between devices: 10.1 us -> none  [on_device(): all_tokens = lax.all_gather(tokens, AXES, axis=0)]
    reduce_sum x4 -> x0, other arithmetic: 3.65 us -> none  [the longest x1 1.15 us: on_device(): jnp.sum(unit * delta_unit, axis=1, keepdims=True)]
    dot_general x3 -> x0, matrix products: 2.75 us -> none  [the longest x1 1.43 us: on_device(): lax.dot_general(unit.astype(bf16), keys, (((1,), (1,)), ((), ())), prefer...]
  transfers between devices with their start and end apart: 3 -> 1, of which waited for: 3 -> 1; matrix products, arithmetic and copies ran while one was open for 3% -> 1% of each run, Pallas kernels for 0% -> 0%
where the time goes in v2:
time: 142 us; the launch traced here: 141 us
  Pallas kernels  80.6 us (57%)
  matrix products  26.9 us (19%)
  waiting for transfers between devices  13.7 us (10%)
  local copies, waits for them, and re-layouts  9.34 us (7%)
  other arithmetic  6.55 us (5%)
  starting transfers between devices  3.53 us (2%)
    pallas_call x1, Pallas kernels, gather(): pl.pallas_call(functools.partial(gather_kernel, n_dp, n_ex), out_shape=(j...  54.4 us
    pallas_call x1, Pallas kernels, loss_grads(): pl.pallas_call(functools.partial(loss_kernel, n_dp, n_ex), out_shape=jax....  26.1 us
    all_to_all x1, waiting for transfers between devices, on_device(): lax.all_to_all(grad_in, 'dp', split_axis=0, concat_axis=1, tiled=True)  13.7 us
    dot_general x1, matrix products, on_device(): lax.dot_general(rows, delta_pre, (((0,), (0,)), ((), ())), preferred_elem...  11.4 us
    dot_general x1, matrix products, on_device(): pre_act = jnp.dot(rows, w_in, preferred_element_type=f32)  3.96 us
    convert_element_type x2, local copies, waits for them, and re-layouts, on_device(): return (grad_in.astype(f32)[None], grad_out[None])  3.78 us
    dot_general x1, matrix products, on_device(): lax.dot_general(place.astype(bf16), all_tokens, (((2,), (1,)), ((0,), (0,...  3.76 us
    all_to_all x1, starting transfers between devices, on_device(): lax.all_to_all(grad_in, 'dp', split_axis=0, concat_axis=1, tiled=True)  3.53 us
  transfers between devices with their start and end apart: 1, of which 1 were waited for; matrix products, arithmetic and copies ran while one was open for 1% of the time, Pallas kernels for 0%

profile of v2, /device:TPU:0, one launch (start us, length us, event | category | flops | bytes accessed | tf_op | source)
XLA Modules:
  0.0 141.4 jit_solution(9531906028437629516)
XLA Ops:
  0.7 1.0 convert_reduce_fusion.own_sum
  1.6 54.4 %shard_map.95 = (bf16[32,128,768]{2,1,0:T(8,128)(2,1)}, f32[32,8,128]{2,1,0:T(8,128)}, bf16[4,2,64,768]{3,2,1,0:T(8,128)(2,1)}) custom-call(bf16[128,768]{1,0:T(8,128)(2,1)} %tok_v.1, bf16[128,768]{1,0:T(8,128)(2,1)} %tok_v.1, s32[2,128]{1,0:T(2,128)} %bitcast.52, bf16[8,768]{1,0:T(8,128)(2,1)} %bitcast.51, bf16[2,64,768]{2,1,0:T(8,128)(2,1)} %bitcast.46), custom_call_target="tpu_custom_call" | custom-call | tf_op jit(solution)/shard_map/pallas_call | solution.py:187
  56.1 0.9 broadcast_compare_fusion
  57.0 0.9 slice.3
  57.9 0.9 fusion.29
  58.8 0.1 broadcast_bitcast_fusion
  58.9 1.4 multiply_reduce_fusion
  60.3 0.1 rsqrt.14.key_scale
  60.3 0.1 fusion.21
  60.5 0.2 fusion.22
  60.7 3.8 %convolution_convert_fusion = bf16[32,64,768]{2,1,0:T(8,128)(2,1)S(1)} fusion(bf16[32,128,768]{2,1,0:T(8,128)(2,1)} %get-tuple-element.6, s32[32,128]{1,0:T(8,128)S(1)} %fusion.21, pred[32,128]{1,0:T(8,128)(4,1)S(1)} %bitcast.50), kind=kOutput, calls=%fused_computation.13 | convolution fusion | flops 404750336 | bytes 9457664 | tf_op jit(solution)/shard_map/dot_general | solution.py:308
  64.5 0.0 copy-start.1
  64.5 0.7 select_reduce_fusion
  65.2 1.1 multiply_convert_fusion.4
  66.3 1.5 %convert_element_type.75 = bf16[2048,64]{0,1:T(8,128)(2,1)S(1)} reshape(bf16[32,64,32,2]{1,0,3,2:T(8,128)(2,1)} %multiply_convert_fusion.4) | data formatting | bytes 524288 | tf_op jit(solution)/shard_map/convert_element_type | solution.py:321
  67.8 0.0 copy-done.1
  67.8 4.0 %fusion.14 = f32[2048,768]{1,0:T(8,128)S(1)} fusion(bf16[2048,768]{1,0:T(8,128)(2,1)S(1)} %bitcast.44, bf16[1,768,3072]{2,1,0:T(8,128)(2,1)} %param.11, s32[]{:T(128)S(6)} %select_n.26), kind=kOutput, calls=%fused_computation.22 | convolution fusion | flops 2415919104 | bytes 10616836 | tf_op jit(solution)/shard_map/dot_general | solution.py:327
  71.8 0.0 copy-start.3
  71.8 2.7 %copy-done.3 = f32[2048,768]{1,0:T(8,128)} copy-done((f32[2048,768]{1,0:T(8,128)}, f32[2048,768]{1,0:T(8,128)S(1)}, u32[]{:S(2)}) %copy-start.3) | copy-done | bytes 6291480
  74.4 0.0 copy-start.2
  74.5 0.0 copy-start
  74.5 2.3 %fusion.20 = bf16[64,768]{1,0:T(8,128)(2,1)S(1)} fusion(bf16[2048,64]{0,1:T(8,128)(2,1)S(1)} %convert_element_type.75, f32[2048,768]{1,0:T(8,128)S(1)} %fusion.14), kind=kOutput, calls=%fused_computation.26 | convolution fusion | flops 215531520 | bytes 6651904 | tf_op jit(solution)/shard_map/dot_general | solution.py:330
  76.8 1.6 %fusion.10 = f32[32,2,768]{2,0,1:T(8,128)S(1)} fusion(bf16[1,3072,768]{2,1,0:T(8,128)(2,1)} %param.12, s32[]{:T(128)S(6)} %select_n.26, bf16[32,2,768]{2,1,0:T(2,128)(2,1)S(1)} %dot_general.33), kind=kOutput, calls=%fused_computation.18 | convolution fusion | flops 75497472 | bytes 1474564 | tf_op jit(solution)/shard_map/dot_general | solution.py:333
  78.4 0.2 copy.18.partial
  78.6 0.0 copy-done.2
  78.6 0.1 dynamic_slice.22
  78.7 0.1 iota_compare_fusion.4
  78.8 0.0 copy-done
  78.8 26.1 %shard_map.96 = f32[32,2,768]{2,1,0:T(2,128)S(1)} custom-call(f32[32,2,768]{2,1,0:T(2,128)S(1)} %copy.18.partial, f32[2,768]{1,0:T(2,128)S(1)} %convert_reduce_fusion.own_sum, bf16[512,768]{1,0:T(8,128)(2,1)S(1)} %bitcast.43, f32[1,512]{1,0:T(1,128)S(1)} %rsqrt.14.key_scale, f32[16,512]{1,0:T(8,128)S(1)} %get-tuple-element.11.include, ...), custom_call_target="tpu_custom_call" | custom-call | tf_op jit(solution)/shard_map/pallas_call | solution.py:272
  104.9 0.1 convert_element_type.79
  105.1 1.8 %fusion.17 = bf16[64,768]{1,0:T(8,128)(2,1)S(1)} fusion(bf16[64,768]{1,0:T(8,128)(2,1)S(1)} %convert_element_type.80, bf16[1,3072,768]{2,1,0:T(8,128)(2,1)} %param.12, s32[]{:T(128)S(6)} %select_n.26), kind=kOutput, calls=%fused_computation.25 | convolution fusion | flops 75546624 | bytes 1376260 | tf_op jit(solution)/shard_map/dot_general | solution.py:349
  106.8 11.4 %fusion.9 = bf16[768,768]{1,0:T(8,128)(2,1)} fusion(bf16[2048,768]{1,0:T(8,128)(2,1)} %bitcast.45, f32[2048,768]{1,0:T(8,128)} %copy-done.3, bf16[2048,64]{0,1:T(8,128)(2,1)S(1)} %convert_element_type.75, bf16[64,768]{1,0:T(8,128)(2,1)S(1)} %fusion.17), kind=kOutput, calls=%fused_computation.17 | convolution fusion | flops 2647719936 | bytes 10977280 | tf_op jit(solution)/shard_map/dot_general | solution.py:353
  118.3 3.5 %all-to-all-start = ((bf16[4,192,768]{2,1,0:T(8,128)(2,1)}), bf16[4,192,768]{2,1,0:T(8,128)(2,1)S(1)}, u32[]{:S(2)}, u32[]{:S(2)}) async-start(bf16[4,192,768]{2,1,0:T(8,128)(2,1)} %bitcast.11), calls=%async_computation | async-start | bytes 2359296 | tf_op jit(solution)/shard_map/all_to_all | solution.py:356
  121.8 1.9 %convolution_bitcast_fusion = f32[1,768,768]{2,1,0:T(8,128)} fusion(bf16[64,768]{1,0:T(8,128)(2,1)S(1)} %fusion.20, bf16[64,768]{1,0:T(8,128)(2,1)S(1)} %convert_element_type.80), kind=kOutput, calls=%fused_computation.15 | convolution fusion | flops 75497472 | bytes 2555904 | tf_op jit(solution)/shard_map/dot_general | solution.py:346
  123.7 13.7 %all-to-all-done = bf16[4,192,768]{2,1,0:T(8,128)(2,1)S(1)} async-done(((bf16[4,192,768]{2,1,0:T(8,128)(2,1)}), bf16[4,192,768]{2,1,0:T(8,128)(2,1)S(1)}, u32[]{:S(2)}, u32[]{:S(2)}) %all-to-all-start) | async-done | bytes 1179680 | tf_op jit(solution)/shard_map/all_to_all | solution.py:356
  137.4 0.2 convert_bitcast_fusion
  137.6 1.5 %copy.19 = f32[192,4,768]{2,1,0:T(4,128)S(1)} copy(f32[192,4,768]{2,0,1:T(8,128)S(1)} %convert_bitcast_fusion) | data formatting | bytes 4718592 | tf_op jit(solution)/shard_map/convert_element_type | solution.py:357
  139.1 2.3 %reshape.130 = f32[1,192,3072]{2,1,0:T(8,128)} reshape(f32[192,4,768]{2,1,0:T(4,128)S(1)} %copy.19) | data formatting | bytes 4718592 | tf_op jit(solution)/shard_map/convert_element_type | solution.py:357
  (9 shorter events, 0.1 us)
Async XLA Ops:
  64.5 3.3 %copy-start.1 = (bf16[32,64,768]{2,1,0:T(8,128)(2,1)}, bf16[32,64,768]{2,1,0:T(8,128)(2,1)S(1)}, u32[]{:S(2)}) copy-start(bf16[32,64,768]{2,1,0:T(8,128)(2,1)S(1)} %convolution_convert_fusion) | copy-start | bytes 9437188
  71.8 2.7 %copy-start.3 = (f32[2048,768]{1,0:T(8,128)}, f32[2048,768]{1,0:T(8,128)S(1)}, u32[]{:S(2)}) copy-start(f32[2048,768]{1,0:T(8,128)S(1)} %fusion.14) | copy-start | bytes 18874372
  74.4 4.1 %copy-start.2 = (s32[64]{0:T(128)S(1)}, s32[64]{0:T(128)}, u32[]{:S(2)}) copy-start(s32[64]{0:T(128)} %param.14) | copy-start | bytes 772
  74.5 4.3 %copy-start = (bf16[4,2,64,768]{3,2,1,0:T(8,128)(2,1)S(1)}, bf16[4,2,64,768]{3,2,1,0:T(8,128)(2,1)}, u32[]{:S(2)}) copy-start(bf16[4,2,64,768]{3,2,1,0:T(8,128)(2,1)} %get-tuple-element.7) | copy-start | bytes 2359300
  118.3 19.1 %all-to-all-start = ((bf16[4,192,768]{2,1,0:T(8,128)(2,1)}), bf16[4,192,768]{2,1,0:T(8,128)(2,1)S(1)}, u32[]{:S(2)}, u32[]{:S(2)}) async-start(bf16[4,192,768]{2,1,0:T(8,128)(2,1)} %bitcast.11), calls=%async_computation | async-start | bytes 2359296 | tf_op jit(solution)/shard_map/all_to_all | solution.py:356

commit v3 on v2

--- a/solution.py
+++ b/solution.py
@@ -283,6 +283,74 @@
     )(partial, own_sum, keys, key_scale, include, pos_hot)
 
 
+def exchange_kernel(n_dp, rows, slope, spread, seq_dh, out, turned, part, local_sem, send_sem, recv_sem):
+    i, e = lax.axis_index("dp"), lax.axis_index("expert")
+    _, parts, keep, wide = out.shape
+    total, width = rows.shape
+    step = 256
+
+    barrier = pltpu.get_barrier_semaphore()
+    for d in range(1, n_dp):
+        pl.semaphore_signal(barrier, inc=1, device_id=(lax.rem(i + d, n_dp), e), device_id_type=MESH)
+
+    def turn(n, _):
+        at = pl.multiple_of(n * step, step)
+        turned[:, pl.ds(at, step)] = rows[pl.ds(at, step), :].T
+        return 0
+
+    lax.fori_loop(0, total // step, turn, 0)
+    pl.semaphore_wait(barrier, n_dp - 1)
+
+    def copy(f, d, slot):
+        t = lax.rem(i + d, n_dp)
+        return pltpu.make_async_remote_copy(
+            src_ref=part.at[f, pl.ds(pl.multiple_of(t * keep, keep), keep), :],
+            dst_ref=out.at[slot, f], send_sem=send_sem.at[f, d], recv_sem=recv_sem.at[f, slot],
+            device_id=(t, e), device_id_type=MESH)
+
+    for f in range(parts):
+        cols = slice(f * wide, (f + 1) * wide)
+        back = jnp.dot(spread[...], seq_dh[:, cols], preferred_element_type=jnp.float32)
+        delta_pre = (back * slope[:, cols].astype(jnp.float32)).astype(jnp.bfloat16)
+        part[f] = jnp.dot(
+            turned[...], delta_pre, preferred_element_type=jnp.float32).astype(jnp.bfloat16)
+        for d in range(1, n_dp):
+            copy(f, d, i).start()
+        pltpu.make_async_copy(
+            part.at[f, pl.ds(pl.multiple_of(i * keep, keep), keep), :], out.at[i, f], local_sem.at[f]
+        ).start()
+    for f in range(parts):
+        pltpu.make_async_copy(
+            part.at[f, pl.ds(pl.multiple_of(i * keep, keep), keep), :], out.at[i, f], local_sem.at[f]
+        ).wait()
+        for d in range(1, n_dp):
+            copy(f, d, lax.rem(i + d, n_dp)).wait_recv()
+            copy(f, d, i).wait_send()
+
+
+def exchange(n_dp, rows, slope, spread, seq_dh):
+    total, width = rows.shape
+    ff = slope.shape[1]
+    wide = 256 if ff % 256 == 0 else ff
+    vmem = pl.BlockSpec(memory_space=pltpu.VMEM)
+    dma = pltpu.SemaphoreType.DMA
+    out = pl.pallas_call(
+        functools.partial(exchange_kernel, n_dp),
+        out_shape=jax.ShapeDtypeStruct((n_dp, ff // wide, width // n_dp, wide), jnp.bfloat16),
+        in_specs=[vmem] * 4,
+        out_specs=vmem,
+        scratch_shapes=[
+            pltpu.VMEM((width, total), jnp.bfloat16),
+            pltpu.VMEM((ff // wide, width, wide), jnp.bfloat16),
+            dma((ff // wide,)), dma((ff // wide, n_dp)), dma((ff // wide, n_dp)),
+        ],
+        compiler_params=pltpu.CompilerParams(
+            collective_id=2, has_side_effects=True, vmem_limit_bytes=56 * 1024 * 1024),
+    )(rows, slope, spread, seq_dh)
+    pieces = [out[j, f] for j in range(n_dp) for f in range(ff // wide)]
+    return jnp.concatenate(pieces, axis=1)
+
+
 def on_device(tokens, expert_ids, router, weight_in, weight_out, premises, positive, tile_mask):
     bf16, f32 = jnp.bfloat16, jnp.float32
     token_count, width = tokens.shape
@@ -326,7 +394,7 @@
     w_out = lax.dynamic_slice_in_dim(weight_out[0], dp * ff, ff, 0)
     pre_act = jnp.dot(rows, w_in, preferred_element_type=f32)
     gelu_val, slope_val = gelu_parts(pre_act)
-    hidden = gelu_val.astype(bf16)
+    hidden, slope = gelu_val.astype(bf16), slope_val.astype(bf16)
     seq_hidden = lax.dot_general(
         spread, hidden, (((0,), (0,)), ((), ())), preferred_element_type=f32
     ).astype(bf16)
@@ -349,11 +417,7 @@
     seq_dh = lax.dot_general(
         delta, w_out, (((1,), (1,)), ((), ())), preferred_element_type=f32
     ).astype(bf16)
-    delta_pre = (jnp.dot(spread, seq_dh, preferred_element_type=f32) * slope_val).astype(bf16)
-    grad_in = lax.dot_general(
-        rows, delta_pre, (((0,), (0,)), ((), ())), preferred_element_type=f32
-    ).astype(bf16)
-    grad_in = lax.all_to_all(grad_in, "dp", split_axis=0, concat_axis=1, tiled=True)
+    grad_in = exchange(n_dp, rows, slope, spread, seq_dh)
     return (grad_in.astype(f32)[None], grad_out[None])
 
 

time: 142 us -> 147 us (1.035)
  Pallas kernels: 80.6 us -> 103 us
  waiting for transfers between devices: 13.7 us -> 0 us
  local copies, waits for them, and re-layouts: 9.34 us -> 14.4 us
  starting transfers between devices: 3.53 us -> 0 us
  matrix products: 26.9 us -> 23.6 us
  other arithmetic: 6.55 us -> 5.03 us
    pallas_call x0 -> x1, Pallas kernels: none -> 22.4 us  [exchange(): pl.pallas_call(functools.partial(exchange_kernel, n_dp), out_shape=jax.Sh...]
    all_to_all x1 -> x0, waiting for transfers between devices: 13.7 us -> none  [on_device(): lax.all_to_all(grad_in, 'dp', split_axis=0, concat_axis=1, tiled=True)]
    dot_general x1 -> x0, matrix products: 11.4 us -> none  [on_device(): lax.dot_general(rows, delta_pre, (((0,), (0,)), ((), ())), preferred_elem...]
    unnamed x9 -> x18, local copies, waits for them, and re-layouts: 2.67 us -> 9.96 us
    dot_general x1, matrix products: 3.96 us -> 9.51 us  [on_device(): pre_act = jnp.dot(rows, w_in, preferred_element_type=f32)]
    convert_element_type x2 -> x0, local copies, waits for them, and re-layouts: 3.78 us -> none  [on_device(): return (grad_in.astype(f32)[None], grad_out[None])]
    all_to_all x1 -> x0, starting transfers between devices: 3.53 us -> none  [on_device(): lax.all_to_all(grad_in, 'dp', split_axis=0, concat_axis=1, tiled=True)]
    dot_general x1, matrix products: 2.32 us -> 4.23 us  [on_device(): lax.dot_general(spread, hidden, (((0,), (0,)), ((), ())), preferred_eleme...]
  transfers between devices with their start and end apart: 1 -> 0, of which waited for: 1 -> 0; matrix products, arithmetic and copies ran while one was open for 1% -> 0% of each run, Pallas kernels for 0% -> 0%
where the time goes in v3:
time: 147 us
  Pallas kernels  103 us (70%)
  matrix products  23.6 us (16%)
  local copies, waits for them, and re-layouts  14.4 us (10%)
  other arithmetic  5.03 us (3%)
    pallas_call x1, Pallas kernels, gather(): pl.pallas_call(functools.partial(gather_kernel, n_dp, n_ex), out_shape=(j...  54.4 us
    pallas_call x1, Pallas kernels, loss_grads(): pl.pallas_call(functools.partial(loss_kernel, n_dp, n_ex), out_shape=jax....  26 us
    pallas_call x1, Pallas kernels, exchange(): pl.pallas_call(functools.partial(exchange_kernel, n_dp), out_shape=jax.Sh...  22.4 us
    unnamed x18, local copies, waits for them, and re-layouts  9.96 us
    dot_general x1, matrix products, on_device(): pre_act = jnp.dot(rows, w_in, preferred_element_type=f32)  9.51 us
    dot_general x1, matrix products, on_device(): lax.dot_general(spread, hidden, (((0,), (0,)), ((), ())), preferred_eleme...  4.23 us
    dot_general x1, matrix products, on_device(): lax.dot_general(place.astype(bf16), all_tokens, (((2,), (1,)), ((0,), (0,...  3.76 us

profile of v3, /device:TPU:0, one launch (start us, length us, event | category | flops | bytes accessed | tf_op | source)
XLA Modules:
  0.0 146.6 jit_solution(16950008824292458604)
XLA Ops:
  0.6 0.7 dynamic_slice.22
  1.4 0.9 fusion.26
  2.2 0.1 broadcast_bitcast_fusion
  2.3 0.1 iota_compare_fusion.4
  2.4 54.4 %shard_map.95 = (bf16[32,128,768]{2,1,0:T(8,128)(2,1)}, f32[32,8,128]{2,1,0:T(8,128)}, bf16[4,2,64,768]{3,2,1,0:T(8,128)(2,1)}) custom-call(bf16[128,768]{1,0:T(8,128)(2,1)} %tok_v.1, bf16[128,768]{1,0:T(8,128)(2,1)} %tok_v.1, s32[2,128]{1,0:T(2,128)} %bitcast.72, bf16[8,768]{1,0:T(8,128)(2,1)} %bitcast.71, bf16[2,64,768]{2,1,0:T(8,128)(2,1)} %bitcast.66), custom_call_target="tpu_custom_call" | custom-call | tf_op jit(solution)/shard_map/pallas_call | solution.py:187
  56.8 0.9 slice.39
  57.8 0.1 fusion.18
  57.9 0.9 broadcast_compare_fusion
  58.8 3.8 %convolution_convert_fusion = bf16[32,64,768]{2,1,0:T(8,128)(2,1)S(1)} fusion(bf16[32,128,768]{2,1,0:T(8,128)(2,1)} %get-tuple-element.6, s32[32,128]{1,0:T(8,128)S(1)} %fusion.18, pred[32,128]{1,0:T(8,128)(4,1)S(1)} %bitcast.69), kind=kOutput, calls=%fused_computation.10 | convolution fusion | flops 404750336 | bytes 9457664 | tf_op jit(solution)/shard_map/dot_general | solution.py:376
  62.6 0.0 copy-start.1
  62.6 9.5 %fusion.5 = (bf16[2048,768]{1,0:T(8,128)(2,1)}, f32[2048,768]{1,0:T(8,128)}) fusion(bf16[2048,768]{1,0:T(8,128)(2,1)S(1)} %bitcast.64, bf16[1,768,3072]{2,1,0:T(8,128)(2,1)} %param.11, s32[]{:T(128)S(6)} %select_n.24), kind=kOutput, calls=%fused_computation.7 | convolution fusion | flops 2444230656 | bytes 13762564 | tf_op jit(solution)/shard_map/dot_general | solution.py:395
  72.1 0.0 copy-done.1
  72.1 0.2 fusion.19
  72.4 0.7 select_reduce_fusion
  73.1 0.2 multiply_convert_fusion.4
  73.3 0.5 convert_element_type.67
  73.7 4.2 %fusion.17 = bf16[64,768]{1,0:T(8,128)(2,1)S(1)} fusion(bf16[2048,64]{0,1:T(8,128)(2,1)S(1)} %convert_element_type.67, f32[2048,768]{1,0:T(8,128)} %get-tuple-element.11), kind=kOutput, calls=%fused_computation.22 | convolution fusion | flops 215531520 | bytes 6651904 | tf_op jit(solution)/shard_map/dot_general | solution.py:398
  78.0 0.0 copy-start
  78.0 0.0 copy-start.2
  78.1 1.7 %fusion.7 = f32[32,2,768]{2,0,1:T(8,128)S(1)} fusion(bf16[1,3072,768]{2,1,0:T(8,128)(2,1)} %param.12, s32[]{:T(128)S(6)} %select_n.24, bf16[32,2,768]{2,1,0:T(2,128)(2,1)S(1)} %dot_general.27), kind=kOutput, calls=%fused_computation.14 | convolution fusion | flops 75497472 | bytes 1474564 | tf_op jit(solution)/shard_map/dot_general | solution.py:401
  79.7 0.2 copy.17.partial
  79.9 0.0 copy-done
  79.9 0.2 multiply_reduce_fusion
  80.1 0.1 rsqrt.14.key_scale
  80.2 0.0 copy-done.2
  80.3 26.0 %shard_map.96 = f32[32,2,768]{2,1,0:T(2,128)S(1)} custom-call(f32[32,2,768]{2,1,0:T(2,128)S(1)} %copy.17.partial, f32[2,768]{1,0:T(2,128)S(1)} %convert_reduce_fusion.own_sum, bf16[512,768]{1,0:T(8,128)(2,1)S(1)} %bitcast.63, f32[1,512]{1,0:T(1,128)S(1)} %rsqrt.14.key_scale, f32[16,512]{1,0:T(8,128)S(1)} %get-tuple-element.13.include, ...), custom_call_target="tpu_custom_call" | custom-call | tf_op jit(solution)/shard_map/pallas_call | solution.py:272
  106.3 0.1 convert_element_type.71
  106.4 1.9 %convolution_bitcast_fusion = f32[1,768,768]{2,1,0:T(8,128)} fusion(bf16[64,768]{1,0:T(8,128)(2,1)S(1)} %fusion.17, bf16[64,768]{1,0:T(8,128)(2,1)S(1)} %convert_element_type.72), kind=kOutput, calls=%fused_computation.12 | convolution fusion | flops 75497472 | bytes 2555904 | tf_op jit(solution)/shard_map/dot_general | solution.py:414
  108.3 2.4 %fusion.14.seq_dh = bf16[64,768]{1,0:T(8,128)(2,1)} fusion(bf16[64,768]{1,0:T(8,128)(2,1)S(1)} %convert_element_type.72, bf16[1,3072,768]{2,1,0:T(8,128)(2,1)} %param.12, s32[]{:T(128)S(6)} %select_n.24), kind=kOutput, calls=%fused_computation.21 | convolution fusion | flops 75546624 | bytes 1376260 | tf_op jit(solution)/shard_map/dot_general | solution.py:417
  110.7 1.0 copy.18.spread
  111.7 22.4 %shard_map.97 = bf16[4,3,192,256]{3,2,1,0:T(8,128)(2,1)} custom-call(bf16[2048,768]{1,0:T(8,128)(2,1)} %bitcast.65, bf16[2048,768]{1,0:T(8,128)(2,1)} %get-tuple-element.10.slope, bf16[2048,64]{1,0:T(8,128)(2,1)} %copy.18.spread, bf16[64,768]{1,0:T(8,128)(2,1)} %fusion.14.seq_dh), custom_call_target="tpu_custom_call" | custom-call | tf_op jit(solution)/shard_map/pallas_call | solution.py:337
  134.1 0.9 bitcast_dynamic-update-slice_fusion.11
  135.0 0.9 bitcast_dynamic-update-slice_fusion.10
  135.9 0.9 bitcast_dynamic-update-slice_fusion.9
  136.8 0.9 bitcast_dynamic-update-slice_fusion.8
  137.7 0.9 bitcast_dynamic-update-slice_fusion.7
  138.6 0.9 bitcast_dynamic-update-slice_fusion.6
  139.6 0.9 bitcast_dynamic-update-slice_fusion.5
  140.5 0.9 bitcast_dynamic-update-slice_fusion.4
  141.4 0.9 bitcast_dynamic-update-slice_fusion.3
  142.3 0.9 bitcast_dynamic-update-slice_fusion.2
  143.2 0.9 bitcast_dynamic-update-slice_fusion.1
  144.1 0.9 bitcast_dynamic-update-slice_fusion
  145.0 1.7 %convert_element_type.74 = f32[1,192,3072]{2,1,0:T(8,128)} convert(bf16[1,192,3072]{2,1,0:T(8,128)(2,1)S(1)} %bitcast_dynamic-update-slice_fusion) | non-fusion elementwise | flops 589824 | bytes 3538944 | tf_op jit(solution)/shard_map/convert_element_type | solution.py:421
  (10 shorter events, 0.2 us)
Async XLA Ops:
  62.6 9.5 %copy-start.1 = (bf16[32,64,768]{2,1,0:T(8,128)(2,1)}, bf16[32,64,768]{2,1,0:T(8,128)(2,1)S(1)}, u32[]{:S(2)}) copy-start(bf16[32,64,768]{2,1,0:T(8,128)(2,1)S(1)} %convolution_convert_fusion) | copy-start | bytes 9437188
  78.0 1.9 %copy-start = (bf16[4,2,64,768]{3,2,1,0:T(8,128)(2,1)S(1)}, bf16[4,2,64,768]{3,2,1,0:T(8,128)(2,1)}, u32[]{:S(2)}) copy-start(bf16[4,2,64,768]{3,2,1,0:T(8,128)(2,1)} %get-tuple-element.7) | copy-start | bytes 2359300
  78.0 2.2 %copy-start.2 = (bf16[128,768]{1,0:T(8,128)(2,1)S(1)}, bf16[128,768]{1,0:T(8,128)(2,1)}, u32[]{:S(2)}) copy-start(bf16[128,768]{1,0:T(8,128)(2,1)} %tok_v.1) | copy-start | bytes 589828

commit v4 on v3

--- a/solution.py
+++ b/solution.py
@@ -40,7 +40,8 @@
 
 
 def gather_kernel(n_dp, n_ex, tok, tok_v, ids, router, prem, all_tok, gates, keys,
-                  gmap, local_sem, send_sem, core_sem, recv_sem, gsend_sem, grecv_sem, psend_sem, precv_sem):
+                  gmap, local_sem, send_sem, core_sem, recv_sem, gsend_sem, grecv_sem, psend_sem, precv_sem,
+                  hsend_sem, hrecv_sem):
     blocks, nz = n_dp * n_ex, n_ex // 2
     i, e = lax.axis_index("dp"), lax.axis_index("expert")
     z, c = e // 2, lax.rem(e, 2)
@@ -61,15 +62,23 @@
     own_keys = pltpu.make_async_copy(prem, keys.at[i], local_sem.at[1])
     own_keys.start()
 
+    square = n_dp == 4
+    peers = 3 if square else n_dp
+
+    def peer(d):
+        if not square:
+            return lax.rem(i + d, n_dp)
+        return (2 - d) * (i + 1 - 2 * lax.rem(i, 2)) + (d - 1) * lax.rem(i + 2, 4)
+
     def own_dp(d, _):
-        move(tok, me, send_sem.at[0, d], (lax.rem(i + d, n_dp), e)).start()
+        move(tok, me, send_sem.at[0, d], (peer(d), e)).start()
         return 0
 
     def own_z(k, _):
         move(tok, me, send_sem.at[k, 0], (i, lax.rem(z + k, nz) * 2 + c)).start()
         return 0
 
-    lax.fori_loop(1, n_dp, own_dp, 0)
+    lax.fori_loop(1, peers, own_dp, 0)
     lax.fori_loop(1, nz, own_z, 0)
     move(tok, me, core_sem.at[me], (i, other)).start()
 
@@ -104,13 +113,29 @@
         move(tok, block, send_sem.at[0, 0], (i, e)).wait_recv()
 
         def on(d, _):
-            move(all_tok.at[block], block, send_sem.at[k, d], (lax.rem(i + d, n_dp), e)).start()
+            move(all_tok.at[block], block, send_sem.at[k, d], (peer(d), e)).start()
             return 0
 
-        lax.fori_loop(1, n_dp, on, 0)
+        lax.fori_loop(1, peers, on, 0)
         move(all_tok.at[block], block, core_sem.at[block], (i, other)).start()
         return 0
 
+    def half_block(block, part, device, k):
+        rows = all_tok.at[block, pl.ds(part * (tok.shape[0] // 2), tok.shape[0] // 2), :]
+        return pltpu.make_async_remote_copy(
+            src_ref=rows, dst_ref=rows, send_sem=hsend_sem.at[k, part], recv_sem=hrecv_sem.at[block, part],
+            device_id=device, device_id_type=MESH)
+
+    def from_dp(n, _):
+        k, d = n // (peers - 1), 1 + lax.rem(n, peers - 1)
+        block = at_block(peer(d), lax.rem(z + k, nz), c)
+        move(tok, block, send_sem.at[0, 0], (i, e)).wait_recv()
+        if square:
+            half_block(block, d - 1, (peer(3 - d), e), k).start()
+        move(all_tok.at[block], block, core_sem.at[block], (i, other)).start()
+        return 0
+
+    lax.fori_loop(0, peers - 1, from_dp, 0)
     lax.fori_loop(1, nz, from_z, 0)
 
     def half(src, row, part, sem, device):
@@ -124,14 +149,17 @@
 
     lax.fori_loop(1, n_dp, own_half, 0)
 
-    def from_dp(n, _):
-        k, d = n // (n_dp - 1), 1 + lax.rem(n, n_dp - 1)
-        block = at_block(lax.rem(i + d, n_dp), lax.rem(z + k, nz), c)
-        move(tok, block, send_sem.at[0, 0], (i, e)).wait_recv()
+    lax.fori_loop(peers - 1, nz * (peers - 1), from_dp, 0)
+
+    def from_diagonal(k, _):
+        block = at_block(3 - i, lax.rem(z + k, nz), c)
+        half_block(block, 0, (i, e), k).wait_recv()
+        half_block(block, 1, (i, e), k).wait_recv()
         move(all_tok.at[block], block, core_sem.at[block], (i, other)).start()
         return 0
 
-    lax.fori_loop(0, nz * (n_dp - 1), from_dp, 0)
+    if square:
+        lax.fori_loop(0, nz, from_diagonal, 0)
 
     def hand_half(d, _):
         row = lax.rem(i + d, n_dp)
@@ -153,11 +181,23 @@
 
     lax.fori_loop(0, n_dp * nz, end_core, 0)
 
-    def end_send(n, _):
-        move(tok, me, send_sem.at[n // n_dp, lax.rem(n, n_dp)], (i, e)).wait_send()
-        return 0
-
-    lax.fori_loop(1, nz * n_dp, end_send, 0)
+    def end_dp(n, _):
+        move(tok, me, send_sem.at[n // (peers - 1), 1 + lax.rem(n, peers - 1)], (i, e)).wait_send()
+        return 0
+
+    def end_z(k, _):
+        move(tok, me, send_sem.at[k, 0], (i, e)).wait_send()
+        return 0
+
+    def end_diagonal(k, _):
+        half_block(me, 0, (i, e), k).wait_send()
+        half_block(me, 1, (i, e), k).wait_send()
+        return 0
+
+    lax.fori_loop(0, nz * (peers - 1), end_dp, 0)
+    lax.fori_loop(1, nz, end_z, 0)
+    if square:
+        lax.fori_loop(0, nz, end_diagonal, 0)
 
     def end_half(d, _):
         half(prem.at[c], lax.rem(i + d, n_dp), 1 - c, d, (i, e)).wait_recv()
@@ -197,6 +237,7 @@
             pltpu.VMEM((router.shape[1], 8, tok), jnp.float32),
             dma((3,)), dma((n_ex // 2, n_dp)), dma((blocks,)), dma((blocks,)),
             dma((blocks,)), dma((blocks,)), dma((2 * n_dp,)), dma((n_dp, 2)),
+            dma((n_ex // 2, 2)), dma((blocks, 2)),
         ],
         compiler_params=pltpu.CompilerParams(collective_id=0, has_side_effects=True),
     )(tokens, tokens, ids.T, router.T, prem)
@@ -283,7 +324,7 @@
     )(partial, own_sum, keys, key_scale, include, pos_hot)
 
 
-def exchange_kernel(n_dp, rows, slope, spread, seq_dh, out, turned, part, local_sem, send_sem, recv_sem):
+def exchange_kernel(n_dp, rows, slope, spread, seq_dh, grads, out, turned, part, local_sem, send_sem, recv_sem):
     i, e = lax.axis_index("dp"), lax.axis_index("expert")
     _, parts, keep, wide = out.shape
     total, width = rows.shape
@@ -325,6 +366,11 @@
         ).wait()
         for d in range(1, n_dp):
             copy(f, d, lax.rem(i + d, n_dp)).wait_recv()
+        for j in range(n_dp):
+            at = (j * parts + f) * wide
+            grads[:, at:at + wide] = out[j, f].astype(jnp.float32)
+    for f in range(parts):
+        for d in range(1, n_dp):
             copy(f, d, i).wait_send()
 
 
@@ -334,12 +380,13 @@
     wide = 256 if ff % 256 == 0 else ff
     vmem = pl.BlockSpec(memory_space=pltpu.VMEM)
     dma = pltpu.SemaphoreType.DMA
-    out = pl.pallas_call(
+    return pl.pallas_call(
         functools.partial(exchange_kernel, n_dp),
-        out_shape=jax.ShapeDtypeStruct((n_dp, ff // wide, width // n_dp, wide), jnp.bfloat16),
+        out_shape=jax.ShapeDtypeStruct((width // n_dp, n_dp * ff), jnp.float32),
         in_specs=[vmem] * 4,
         out_specs=vmem,
         scratch_shapes=[
+            pltpu.VMEM((n_dp, ff // wide, width // n_dp, wide), jnp.bfloat16),
             pltpu.VMEM((width, total), jnp.bfloat16),
             pltpu.VMEM((ff // wide, width, wide), jnp.bfloat16),
             dma((ff // wide,)), dma((ff // wide, n_dp)), dma((ff // wide, n_dp)),
@@ -347,8 +394,6 @@
         compiler_params=pltpu.CompilerParams(
             collective_id=2, has_side_effects=True, vmem_limit_bytes=56 * 1024 * 1024),
     )(rows, slope, spread, seq_dh)
-    pieces = [out[j, f] for j in range(n_dp) for f in range(ff // wide)]
-    return jnp.concatenate(pieces, axis=1)
 
 
 def on_device(tokens, expert_ids, router, weight_in, weight_out, premises, positive, tile_mask):

time: 147 us -> 132 us (0.90)
  local copies, waits for them, and re-layouts: 14.4 us -> 6.82 us
  Pallas kernels: 103 us -> 97.4 us
  other arithmetic: 5.03 us -> 3.37 us
    unnamed x18 -> x8, local copies, waits for them, and re-layouts: 9.96 us -> 3.32 us
    pallas_call x1, Pallas kernels: 54.4 us -> 48.9 us  [gather(): pl.pallas_call(functools.partial(gather_kernel, n_dp, n_ex), out_shape=(j...]
    convert_element_type x1 -> x0, other arithmetic: 1.67 us -> none  [on_device(): return (grad_in.astype(f32)[None], grad_out[None])]
where the time goes in v4:
time: 132 us
  Pallas kernels  97.4 us (74%)
  matrix products  23.6 us (18%)
  local copies, waits for them, and re-layouts  6.82 us (5%)
  other arithmetic  3.37 us (3%)
    pallas_call x1, Pallas kernels, gather(): pl.pallas_call(functools.partial(gather_kernel, n_dp, n_ex), out_shape=(j...  48.9 us
    pallas_call x1, Pallas kernels, loss_grads(): pl.pallas_call(functools.partial(loss_kernel, n_dp, n_ex), out_shape=jax....  25.8 us
    pallas_call x1, Pallas kernels, exchange(): pl.pallas_call(functools.partial(exchange_kernel, n_dp), out_shape=jax.Sh...  22.7 us
    dot_general x1, matrix products, on_device(): pre_act = jnp.dot(rows, w_in, preferred_element_type=f32)  9.52 us
    dot_general x1, matrix products, on_device(): lax.dot_general(spread, hidden, (((0,), (0,)), ((), ())), preferred_eleme...  4.31 us
    dot_general x1, matrix products, on_device(): lax.dot_general(place.astype(bf16), all_tokens, (((2,), (1,)), ((0,), (0,...  3.76 us
    unnamed x8, local copies, waits for them, and re-layouts  3.32 us

profile of v4, /device:TPU:0, one launch (start us, length us, event | category | flops | bytes accessed | tf_op | source)
XLA Modules:
  0.0 132.0 jit_solution(17625724640439956053)
XLA Ops:
  0.6 0.7 dynamic_slice.22
  1.4 0.9 fusion.26
  2.2 0.1 broadcast_bitcast_fusion
  2.3 0.1 iota_compare_fusion.4
  2.4 48.9 %shard_map.95 = (bf16[32,128,768]{2,1,0:T(8,128)(2,1)}, f32[32,8,128]{2,1,0:T(8,128)}, bf16[4,2,64,768]{3,2,1,0:T(8,128)(2,1)}) custom-call(bf16[128,768]{1,0:T(8,128)(2,1)} %tok_v.1, bf16[128,768]{1,0:T(8,128)(2,1)} %tok_v.1, s32[2,128]{1,0:T(2,128)} %bitcast.50, bf16[8,768]{1,0:T(8,128)(2,1)} %bitcast.49, bf16[2,64,768]{2,1,0:T(8,128)(2,1)} %bitcast.44), custom_call_target="tpu_custom_call" | custom-call | tf_op jit(solution)/shard_map/pallas_call | solution.py:227
  51.3 0.9 slice.3
  52.2 0.1 fusion.18
  52.4 0.9 broadcast_compare_fusion
  53.3 3.8 %convolution_convert_fusion = bf16[32,64,768]{2,1,0:T(8,128)(2,1)S(1)} fusion(bf16[32,128,768]{2,1,0:T(8,128)(2,1)} %get-tuple-element.6, s32[32,128]{1,0:T(8,128)S(1)} %fusion.18, pred[32,128]{1,0:T(8,128)(4,1)S(1)} %bitcast.47), kind=kOutput, calls=%fused_computation.10 | convolution fusion | flops 404750336 | bytes 9457664 | tf_op jit(solution)/shard_map/dot_general | solution.py:421
  57.1 0.0 copy-start.1
  57.1 9.5 %fusion.5 = (bf16[2048,768]{1,0:T(8,128)(2,1)}, f32[2048,768]{1,0:T(8,128)}) fusion(bf16[2048,768]{1,0:T(8,128)(2,1)S(1)} %bitcast.41, bf16[1,768,3072]{2,1,0:T(8,128)(2,1)} %param.11, s32[]{:T(128)S(6)} %select_n.24), kind=kOutput, calls=%fused_computation.7 | convolution fusion | flops 2444230656 | bytes 13762564 | tf_op jit(solution)/shard_map/dot_general | solution.py:440
  66.6 0.0 copy-done.1
  66.6 0.2 fusion.19
  66.9 0.7 select_reduce_fusion
  67.6 0.2 multiply_convert_fusion.4
  67.8 0.5 convert_element_type.57
  68.2 0.0 copy-start
  68.2 0.0 copy-start.2
  68.3 4.3 %fusion.17 = bf16[64,768]{1,0:T(8,128)(2,1)S(1)} fusion(bf16[2048,64]{0,1:T(8,128)(2,1)S(1)} %convert_element_type.57, f32[2048,768]{1,0:T(8,128)} %get-tuple-element.11), kind=kOutput, calls=%fused_computation.22 | convolution fusion | flops 215531520 | bytes 6651904 | tf_op jit(solution)/shard_map/dot_general | solution.py:443
  72.6 1.6 %fusion.7 = f32[32,2,768]{2,0,1:T(8,128)S(1)} fusion(bf16[1,3072,768]{2,1,0:T(8,128)(2,1)} %param.12, s32[]{:T(128)S(6)} %select_n.24, bf16[32,2,768]{2,1,0:T(2,128)(2,1)S(1)} %dot_general.27), kind=kOutput, calls=%fused_computation.14 | convolution fusion | flops 75497472 | bytes 1474564 | tf_op jit(solution)/shard_map/dot_general | solution.py:446
  74.2 0.2 copy.17.partial
  74.4 0.0 copy-done
  74.4 0.2 multiply_reduce_fusion
  74.6 0.1 rsqrt.14.key_scale
  74.7 0.0 copy-done.2
  74.8 25.8 %shard_map.96 = f32[32,2,768]{2,1,0:T(2,128)S(1)} custom-call(f32[32,2,768]{2,1,0:T(2,128)S(1)} %copy.17.partial, f32[2,768]{1,0:T(2,128)S(1)} %convert_reduce_fusion.own_sum, bf16[512,768]{1,0:T(8,128)(2,1)S(1)} %bitcast.40, f32[1,512]{1,0:T(1,128)S(1)} %rsqrt.14.key_scale, f32[16,512]{1,0:T(8,128)S(1)} %get-tuple-element.13.include, ...), custom_call_target="tpu_custom_call" | custom-call | tf_op jit(solution)/shard_map/pallas_call | solution.py:313
  100.6 0.1 convert_element_type.61
  100.7 1.9 %convolution_bitcast_fusion = f32[1,768,768]{2,1,0:T(8,128)} fusion(bf16[64,768]{1,0:T(8,128)(2,1)S(1)} %fusion.17, bf16[64,768]{1,0:T(8,128)(2,1)S(1)} %convert_element_type.62), kind=kOutput, calls=%fused_computation.12 | convolution fusion | flops 75497472 | bytes 2555904 | tf_op jit(solution)/shard_map/dot_general | solution.py:459
  102.6 2.4 %fusion.14.seq_dh = bf16[64,768]{1,0:T(8,128)(2,1)} fusion(bf16[64,768]{1,0:T(8,128)(2,1)S(1)} %convert_element_type.62, bf16[1,3072,768]{2,1,0:T(8,128)(2,1)} %param.12, s32[]{:T(128)S(6)} %select_n.24), kind=kOutput, calls=%fused_computation.21 | convolution fusion | flops 75546624 | bytes 1376260 | tf_op jit(solution)/shard_map/dot_general | solution.py:462
  105.0 1.0 copy.18.spread
  106.0 22.7 %shard_map.97 = f32[192,3072]{1,0:T(8,128)} custom-call(bf16[2048,768]{1,0:T(8,128)(2,1)} %bitcast.42, bf16[2048,768]{1,0:T(8,128)(2,1)} %get-tuple-element.10.slope, bf16[2048,64]{1,0:T(8,128)(2,1)} %copy.18.spread, bf16[64,768]{1,0:T(8,128)(2,1)} %fusion.14.seq_dh), custom_call_target="tpu_custom_call" | custom-call | tf_op jit(solution)/shard_map/pallas_call | solution.py:383
  128.7 3.3 %copy.25 = f32[1,192,3072]{2,1,0:T(8,128)} copy(f32[1,192,3072]{2,1,0:T(8,128)} %bitcast.43) | data formatting | bytes 4718592
  (10 shorter events, 0.2 us)
Async XLA Ops:
  57.1 9.5 %copy-start.1 = (bf16[32,64,768]{2,1,0:T(8,128)(2,1)}, bf16[32,64,768]{2,1,0:T(8,128)(2,1)S(1)}, u32[]{:S(2)}) copy-start(bf16[32,64,768]{2,1,0:T(8,128)(2,1)S(1)} %convolution_convert_fusion) | copy-start | bytes 9437188
  68.2 6.2 %copy-start = (bf16[4,2,64,768]{3,2,1,0:T(8,128)(2,1)S(1)}, bf16[4,2,64,768]{3,2,1,0:T(8,128)(2,1)}, u32[]{:S(2)}) copy-start(bf16[4,2,64,768]{3,2,1,0:T(8,128)(2,1)} %get-tuple-element.7) | copy-start | bytes 2359300
  68.2 6.5 %copy-start.2 = (bf16[128,768]{1,0:T(8,128)(2,1)S(1)}, bf16[128,768]{1,0:T(8,128)(2,1)}, u32[]{:S(2)}) copy-start(bf16[128,768]{1,0:T(8,128)(2,1)} %tok_v.1) | copy-start | bytes 589828

commit v5 on v4

--- a/solution.py
+++ b/solution.py
@@ -368,7 +368,7 @@
             copy(f, d, lax.rem(i + d, n_dp)).wait_recv()
         for j in range(n_dp):
             at = (j * parts + f) * wide
-            grads[:, at:at + wide] = out[j, f].astype(jnp.float32)
+            grads[:, at:at + wide] = out[j, f]
     for f in range(parts):
         for d in range(1, n_dp):
             copy(f, d, i).wait_send()
@@ -382,7 +382,7 @@
     dma = pltpu.SemaphoreType.DMA
     return pl.pallas_call(
         functools.partial(exchange_kernel, n_dp),
-        out_shape=jax.ShapeDtypeStruct((width // n_dp, n_dp * ff), jnp.float32),
+        out_shape=jax.ShapeDtypeStruct((width // n_dp, n_dp * ff), jnp.bfloat16),
         in_specs=[vmem] * 4,
         out_specs=vmem,
         scratch_shapes=[
@@ -439,7 +439,7 @@
     w_out = lax.dynamic_slice_in_dim(weight_out[0], dp * ff, ff, 0)
     pre_act = jnp.dot(rows, w_in, preferred_element_type=f32)
     gelu_val, slope_val = gelu_parts(pre_act)
-    hidden, slope = gelu_val.astype(bf16), slope_val.astype(bf16)
+    hidden, slope = lax.optimization_barrier((gelu_val.astype(bf16), slope_val.astype(bf16)))
     seq_hidden = lax.dot_general(
         spread, hidden, (((0,), (0,)), ((), ())), preferred_element_type=f32
     ).astype(bf16)

time: 132 us -> 130 us (0.985)
  local copies, waits for them, and re-layouts: 6.82 us -> 3.53 us
  other arithmetic: 3.37 us -> 6.3 us
  matrix products: 23.6 us -> 21.9 us
    unnamed x8 -> x7, local copies, waits for them, and re-layouts: 3.32 us -> 0.02 us
    broadcast_in_dim x0 -> x1, other arithmetic: none -> 2.94 us  [on_device(): return (grad_in.astype(f32)[None], grad_out[None])]
    dot_general x1, matrix products: 4.31 us -> 2.53 us  [on_device(): lax.dot_general(spread, hidden, (((0,), (0,)), ((), ())), preferred_eleme...]
where the time goes in v5:
time: 130 us
  Pallas kernels  97 us (75%)
  matrix products  21.9 us (17%)
  other arithmetic  6.3 us (5%)
  local copies, waits for them, and re-layouts  3.53 us (3%)
    pallas_call x1, Pallas kernels, gather(): pl.pallas_call(functools.partial(gather_kernel, n_dp, n_ex), out_shape=(j...  48.9 us
    pallas_call x1, Pallas kernels, loss_grads(): pl.pallas_call(functools.partial(loss_kernel, n_dp, n_ex), out_shape=jax....  25.8 us
    pallas_call x1, Pallas kernels, exchange(): pl.pallas_call(functools.partial(exchange_kernel, n_dp), out_shape=jax.Sh...  22.3 us
    dot_general x1, matrix products, on_device(): pre_act = jnp.dot(rows, w_in, preferred_element_type=f32)  9.58 us
    dot_general x1, matrix products, on_device(): lax.dot_general(place.astype(bf16), all_tokens, (((2,), (1,)), ((0,), (0,...  3.76 us
    broadcast_in_dim x1, other arithmetic, on_device(): return (grad_in.astype(f32)[None], grad_out[None])  2.94 us

profile of v5, /device:TPU:0, one launch (start us, length us, event | category | flops | bytes accessed | tf_op | source)
XLA Modules:
  0.0 129.5 jit_solution(11393984966656443129)
XLA Ops:
  0.6 0.7 dynamic_slice.22
  1.4 0.9 fusion.24
  2.2 0.1 broadcast_bitcast_fusion
  2.3 0.1 iota_compare_fusion.4
  2.4 48.9 %shard_map.95 = (bf16[32,128,768]{2,1,0:T(8,128)(2,1)}, f32[32,8,128]{2,1,0:T(8,128)}, bf16[4,2,64,768]{3,2,1,0:T(8,128)(2,1)}) custom-call(bf16[128,768]{1,0:T(8,128)(2,1)} %tok_v.1, bf16[128,768]{1,0:T(8,128)(2,1)} %tok_v.1, s32[2,128]{1,0:T(2,128)} %bitcast.52, bf16[8,768]{1,0:T(8,128)(2,1)} %bitcast.51, bf16[2,64,768]{2,1,0:T(8,128)(2,1)} %bitcast.46), custom_call_target="tpu_custom_call" | custom-call | tf_op jit(solution)/shard_map/pallas_call | solution.py:227
  51.3 0.9 slice.3
  52.2 0.1 fusion.16
  52.4 0.9 broadcast_compare_fusion
  53.3 3.8 %convolution_convert_fusion = bf16[32,64,768]{2,1,0:T(8,128)(2,1)S(1)} fusion(bf16[32,128,768]{2,1,0:T(8,128)(2,1)} %get-tuple-element.8, s32[32,128]{1,0:T(8,128)S(1)} %fusion.16, pred[32,128]{1,0:T(8,128)(4,1)S(1)} %bitcast.49), kind=kOutput, calls=%fused_computation.9 | convolution fusion | flops 404750336 | bytes 9457664 | tf_op jit(solution)/shard_map/dot_general | solution.py:421
  57.1 0.0 copy-start.1
  57.1 9.6 %fusion.5 = (bf16[2048,768]{1,0:T(8,128)(2,1)}, bf16[2048,768]{1,0:T(8,128)(2,1)}) fusion(bf16[2048,768]{1,0:T(8,128)(2,1)S(1)} %bitcast.44, bf16[1,768,3072]{2,1,0:T(8,128)(2,1)} %param.11, s32[]{:T(128)S(6)} %select_n.24), kind=kOutput, calls=%fused_computation.7 | convolution fusion | flops 2447376384 | bytes 10616836 | tf_op jit(solution)/shard_map/dot_general | solution.py:440
  66.7 0.0 copy-done.1
  66.7 0.0 copy-start
  66.7 0.0 copy-start.2
  66.7 0.2 fusion.17
  66.9 0.7 select_reduce_fusion
  67.6 0.2 multiply_convert_fusion.1
  67.9 0.5 convert_element_type.59
  68.3 2.5 %convolution_convert_fusion.1 = bf16[64,768]{1,0:T(8,128)(2,1)S(1)} fusion(bf16[2048,64]{0,1:T(8,128)(2,1)S(1)} %convert_element_type.59, bf16[2048,768]{1,0:T(8,128)(2,1)} %get-tuple-element.10), kind=kOutput, calls=%fused_computation.22 | convolution fusion | flops 201375744 | bytes 3506176 | tf_op jit(solution)/shard_map/dot_general | solution.py:443
  70.9 1.6 %fusion.6 = f32[32,2,768]{2,0,1:T(8,128)S(1)} fusion(bf16[1,3072,768]{2,1,0:T(8,128)(2,1)} %param.12, s32[]{:T(128)S(6)} %select_n.24, bf16[32,2,768]{2,1,0:T(2,128)(2,1)S(1)} %dot_general.27), kind=kOutput, calls=%fused_computation.14 | convolution fusion | flops 75497472 | bytes 1474564 | tf_op jit(solution)/shard_map/dot_general | solution.py:446
  72.5 0.2 copy.17.partial
  72.6 0.0 copy-done
  72.7 0.2 multiply_reduce_fusion
  72.9 0.1 rsqrt.14.key_scale
  73.0 0.0 copy-done.2
  73.0 25.8 %shard_map.96 = f32[32,2,768]{2,1,0:T(2,128)S(1)} custom-call(f32[32,2,768]{2,1,0:T(2,128)S(1)} %copy.17.partial, f32[2,768]{1,0:T(2,128)S(1)} %convert_reduce_fusion.own_sum, bf16[512,768]{1,0:T(8,128)(2,1)S(1)} %bitcast.43, f32[1,512]{1,0:T(1,128)S(1)} %rsqrt.14.key_scale, f32[16,512]{1,0:T(8,128)S(1)} %get-tuple-element.17.include, ...), custom_call_target="tpu_custom_call" | custom-call | tf_op jit(solution)/shard_map/pallas_call | solution.py:313
  98.8 0.1 convert_element_type.62
  99.0 1.9 %convolution_bitcast_fusion = f32[1,768,768]{2,1,0:T(8,128)} fusion(bf16[64,768]{1,0:T(8,128)(2,1)S(1)} %convolution_convert_fusion.1, bf16[64,768]{1,0:T(8,128)(2,1)S(1)} %convert_element_type.63), kind=kOutput, calls=%fused_computation.11 | convolution fusion | flops 75497472 | bytes 2555904 | tf_op jit(solution)/shard_map/dot_general | solution.py:459
  100.9 2.4 %fusion.13.seq_dh = bf16[64,768]{1,0:T(8,128)(2,1)} fusion(bf16[64,768]{1,0:T(8,128)(2,1)S(1)} %convert_element_type.63, bf16[1,3072,768]{2,1,0:T(8,128)(2,1)} %param.12, s32[]{:T(128)S(6)} %select_n.24), kind=kOutput, calls=%fused_computation.21 | convolution fusion | flops 75546624 | bytes 1376260 | tf_op jit(solution)/shard_map/dot_general | solution.py:462
  103.3 1.0 copy.18.spread
  104.3 22.3 %shard_map.97 = bf16[192,3072]{1,0:T(8,128)(2,1)} custom-call(bf16[2048,768]{1,0:T(8,128)(2,1)} %bitcast.45, bf16[2048,768]{1,0:T(8,128)(2,1)} %get-tuple-element.9.slope, bf16[2048,64]{1,0:T(8,128)(2,1)} %copy.18.spread, bf16[64,768]{1,0:T(8,128)(2,1)} %fusion.13.seq_dh), custom_call_target="tpu_custom_call" | custom-call | tf_op jit(solution)/shard_map/pallas_call | solution.py:383
  126.6 2.9 %bitcast_convert_fusion = f32[1,192,3072]{2,1,0:T(8,128)} fusion(bf16[192,3072]{1,0:T(8,128)(2,1)} %shard_map.97), kind=kLoop, calls=%fused_computation.13 | loop fusion | flops 589824 | bytes 3538944 | tf_op jit(solution)/shard_map/broadcast_in_dim | solution.py:466
  (10 shorter events, 0.2 us)
Async XLA Ops:
  57.1 9.6 %copy-start.1 = (bf16[32,64,768]{2,1,0:T(8,128)(2,1)}, bf16[32,64,768]{2,1,0:T(8,128)(2,1)S(1)}, u32[]{:S(2)}) copy-start(bf16[32,64,768]{2,1,0:T(8,128)(2,1)S(1)} %convolution_convert_fusion) | copy-start | bytes 9437188
  66.7 6.0 %copy-start = (bf16[4,2,64,768]{3,2,1,0:T(8,128)(2,1)S(1)}, bf16[4,2,64,768]{3,2,1,0:T(8,128)(2,1)}, u32[]{:S(2)}) copy-start(bf16[4,2,64,768]{3,2,1,0:T(8,128)(2,1)} %get-tuple-element.11) | copy-start | bytes 2359300
  66.7 6.3 %copy-start.2 = (bf16[128,768]{1,0:T(8,128)(2,1)S(1)}, bf16[128,768]{1,0:T(8,128)(2,1)}, u32[]{:S(2)}) copy-start(bf16[128,768]{1,0:T(8,128)(2,1)} %tok_v.1) | copy-start | bytes 589828
